TPU v7x, 32 devices: a whole 2x2x4 slice. The times are simulated.
32 devices in a mesh: mesh: 8 (over z, x), bg: 4 (over y, core).
Axes of the slice: x: 2, y: 2, z: 4, core: 2. Of those that a mesh axis runs over, the one named last changes fastest.
Arguments:
- displacement: float32 [3, 32, 16, 128], P(None, 'mesh', 'bg'), may hold values from -0.4 to 0.4
- bg_coef: float32 [8, 524288], P(None, ('mesh', 'bg')), may hold values from -0.3 to 0.3
- query_elem: int32 [32, 32, 544], P(('mesh', 'bg')), may hold values from 0 to 16383
- query_point: int32 [32, 32, 544], P(('mesh', 'bg')), may hold values from 0 to 6912, as said below
- query_coord: float32 [32, 32, 3, 544], P(('mesh', 'bg')), may hold values from 0 to 1
Outputs:
- new_displacement: float32 [3, 32, 16, 128], P(None, 'mesh', 'bg')
- line_coeffs: float32 [2, 5], replicated
Inputs may be any that keep to these rules, and one draw needn't show every extreme that they name: `query_point`: in each row every quadrature point 0 to 6911 of the row's device fills exactly one slot; all other slots hold 6912 and are empty. In every draw some owner's bucket is full in every row.
All inputs are finite; a program needn't handle non-finite values.
Results may differ from a plain program's by a relative error of at most 0.0003.
Values sent between devices are 32-bit elements; how exact they have to be, the bound alone decides.
A program may use at most 64 MiB of HBM per device.

v0:
```python
import jax
import jax.numpy as jnp
import numpy as np
from jax import lax
from jax.sharding import PartitionSpec as P

PASSES = 2
LS_STEPS = 4


GAUSS_POINTS = np.array([0.5 - 0.5 * np.sqrt(0.6), 0.5, 0.5 + 0.5 * np.sqrt(0.6)])
GAUSS_WEIGHTS = np.array([5.0 / 18.0, 8.0 / 18.0, 5.0 / 18.0])


def extended(block, sides, width):
    for axis, dim in sides:
        count = lax.axis_size(axis)
        forward = [(i, i + 1) for i in range(count - 1)]
        forward.append((count - 1, 0))
        backward = [(target, source) for source, target in forward]
        low = lax.ppermute(
            lax.slice_in_dim(block, block.shape[dim] - width, None, axis=dim), axis, forward
        )
        high = lax.ppermute(lax.slice_in_dim(block, 0, width, axis=dim), axis, backward)
        block = jnp.concatenate([low, block, high], axis=dim)
    return block


def basis_tables(elements, periodic):
    node_count = 2 * elements if periodic else 2 * elements + 1
    values = np.zeros((node_count, 3 * elements))
    slopes = np.zeros((node_count, 3 * elements))
    points = GAUSS_POINTS
    shape_values = [
        2.0 * (points - 0.5) * (points - 1.0),
        -4.0 * points * (points - 1.0),
        2.0 * points * (points - 0.5),
    ]
    shape_slopes = [4.0 * points - 3.0, 4.0 - 8.0 * points, 4.0 * points - 1.0]
    for offset in range(3):
        node_rows = (2 * np.arange(elements) + offset) % node_count
        for gauss_index in range(3):
            columns = 3 * np.arange(elements) + gauss_index
            values[node_rows, columns] += shape_values[offset][gauss_index]
            slopes[node_rows, columns] += shape_slopes[offset][gauss_index]
    return (jnp.asarray(values, dtype=jnp.float32), jnp.asarray(slopes, dtype=jnp.float32))


def quad_weights(z_elems, y_elems, x_elems):
    along_z = jnp.asarray(np.tile(GAUSS_WEIGHTS, z_elems), dtype=jnp.float32)
    along_y = jnp.asarray(np.tile(GAUSS_WEIGHTS, y_elems), dtype=jnp.float32)
    along_x = jnp.asarray(np.tile(GAUSS_WEIGHTS, x_elems), dtype=jnp.float32)
    return along_z[:, None, None] * along_y[None, :, None] * along_x[None, None, :]


def gradients(node_field, tables):
    z_value, z_slope, y_value, y_slope, value_along_x, x_slope = tables
    highest = lax.Precision.HIGHEST
    value_z = jnp.einsum("czyx,zk->ckyx", node_field, z_value, precision=highest)
    slope_z = jnp.einsum("czyx,zk->ckyx", node_field, z_slope, precision=highest)
    value_zy = jnp.einsum("ckyx,yl->cklx", value_z, y_value, precision=highest)
    slope_y = jnp.einsum("ckyx,yl->cklx", value_z, y_slope, precision=highest)
    slope_zy = jnp.einsum("ckyx,yl->cklx", slope_z, y_value, precision=highest)
    deriv_x = jnp.einsum("cklx,xm->cklm", value_zy, x_slope, precision=highest)
    deriv_y = jnp.einsum("cklx,xm->cklm", slope_y, value_along_x, precision=highest)
    deriv_z = jnp.einsum("cklx,xm->cklm", slope_zy, value_along_x, precision=highest)
    return jnp.stack([deriv_x, deriv_y, deriv_z], axis=1)


def identity_block():
    return jnp.eye(3, dtype=jnp.float32)[:, :, None, None, None]


def gram(left_part, right_part):
    return jnp.sum(left_part[:, :, None] * right_part[:, None, :], axis=0)


def energy(node_field, tables, target_size_scale, weights):
    jacobian = gradients(node_field, tables) + identity_block()
    strain = gram(jacobian, jacobian) * target_size_scale - identity_block()
    return jnp.sum(weights * jnp.sum(strain * strain, axis=(0, 1)))


def line_terms(node_field, direction, tables, target_size_scale, weights):
    jacobian = gradients(node_field, tables) + identity_block()
    motion = gradients(direction, tables)
    strain_zero = gram(jacobian, jacobian) * target_size_scale - identity_block()
    mixed = gram(jacobian, motion)
    strain_one = (mixed + jnp.swapaxes(mixed, 0, 1)) * target_size_scale
    strain_two = gram(motion, motion) * target_size_scale

    def weighted(first_part, latter_portion):
        return jnp.sum(weights * jnp.sum(first_part * latter_portion, axis=(0, 1)))

    zero_zero = weighted(strain_zero, strain_zero)
    zero_one = weighted(strain_zero, strain_one)
    zero_two = weighted(strain_zero, strain_two)
    one_two = weighted(strain_one, strain_two)
    two_two = weighted(strain_two, strain_two)
    gauss_newton = weighted(strain_one, strain_one)
    return (
        zero_zero,
        2.0 * zero_one,
        gauss_newton + 2.0 * zero_two,
        2.0 * one_two,
        two_two,
        gauss_newton,
    )


def line_search(terms):
    const_term, linear, quadratic, cubic_term, quartic, gauss_newton = terms
    step_len = jnp.zeros((), jnp.float32)
    for search_turn in range(LS_STEPS):
        slope = linear + step_len * (
            2.0 * quadratic + step_len * (3.0 * cubic_term + step_len * 4.0 * quartic)
        )
        curvature = 2.0 * quadratic + step_len * (6.0 * cubic_term + step_len * 12.0 * quartic)
        step_len = step_len - slope / jnp.maximum(curvature, gauss_newton + 1e-06)
    return step_len


def inverse_square(coefs, coords):
    along_x = coords[:, 0]
    along_y = coords[:, 1]
    along_z = coords[:, 2]
    summed = jnp.zeros_like(along_x)
    for corner in range(8):
        weight_x = along_x if corner & 1 else 1.0 - along_x
        weight_y = along_y if corner & 2 else 1.0 - along_y
        weight_z = along_z if corner & 4 else 1.0 - along_z
        summed = summed + weight_x * weight_y * weight_z * coefs[:, corner]
    return jnp.exp(-2.0 * summed)


def gather_coefs(table, elem_ids):
    index_rows = elem_ids[:, 0, :]
    corner_rows = jnp.take(jnp.transpose(table), index_rows, axis=0)
    return jnp.moveaxis(corner_rows, 2, 1)


def answer(reply):
    return lax.all_to_all(reply, ("mesh", "bg"), split_axis=0, concat_axis=0, tiled=True)


def assemble(local_part):
    padded_z = extended(local_part, (("mesh", 1),), 1)
    partial_sum = local_part.at[:, 0].add(padded_z[:, 0]).at[:, -1].add(padded_z[:, -1])
    padded_y = extended(partial_sum, (("bg", 2),), 1)
    summed = partial_sum.at[:, :, 0].add(padded_y[:, :, 0]).at[:, :, -1].add(padded_y[:, :, -1])
    return summed


def shards(displacement, bg_coef, query_elem, query_point, query_coord):
    devices = lax.axis_size("mesh") * lax.axis_size("bg")
    z_elems = displacement.shape[1] // 2
    y_elems = displacement.shape[2] // 2
    x_elems = displacement.shape[3] // 2
    tables = (
        basis_tables(z_elems, False) + basis_tables(y_elems, False) + basis_tables(x_elems, True)
    )
    weights = quad_weights(z_elems, y_elems, x_elems)
    point_count = 27 * z_elems * y_elems * x_elems
    elem_ids = query_elem.reshape(devices, 1, -1)
    coords = query_coord.reshape(devices, 3, -1)
    found_vals = answer(
        inverse_square(
            gather_coefs(
                bg_coef,
                lax.all_to_all(elem_ids, ("mesh", "bg"), split_axis=0, concat_axis=0, tiled=True),
            ),
            lax.all_to_all(coords, ("mesh", "bg"), split_axis=0, concat_axis=0, tiled=True),
        )[:, None, :]
    ).reshape(-1)
    target_size_scale = (
        jnp.zeros((point_count,), jnp.float32)
        .at[query_point.reshape(-1)]
        .set(found_vals, mode="drop")
    )
    target_size_scale = target_size_scale.reshape(3 * z_elems, 3 * y_elems, 3 * x_elems)

    def local_energy(values):
        return energy(values, tables, target_size_scale, weights)

    node_field = assemble(jnp.pad(displacement, ((0, 0), (0, 1), (0, 1), (0, 0))))
    history = []
    for newton_pass in range(PASSES):
        direction = -assemble(jax.grad(local_energy)(node_field))
        partial_terms = jnp.stack(
            line_terms(node_field, direction, tables, target_size_scale, weights)
        )
        totals = lax.psum(partial_terms, ("mesh", "bg"))
        step_len = line_search(totals)
        node_field = node_field + step_len * direction
        history.append(totals[:5] / (devices * z_elems * y_elems * x_elems))
    return (node_field[:, :-1, :-1], jnp.stack(history))


def solution(mesh):
    in_specs = (
        P(None, "mesh", "bg", None),
        P(None, ("mesh", "bg")),
        P(("mesh", "bg"), None, None),
        P(("mesh", "bg"), None, None),
        P(("mesh", "bg"), None, None, None),
    )
    out_specs = (P(None, "mesh", "bg", None), P())
    return jax.shard_map(shards, mesh=mesh, in_specs=in_specs, out_specs=out_specs, check_vma=False)
```

profile of v0, /device:TPU:0, one launch (start us, length us, event | category | flops | bytes accessed | tf_op | source)
XLA Modules:
  0.0 336.7 jit_solution(7580339313714146520)
XLA Ops:
  0.7 3.0 collective-permute-start
  3.6 1.6 reshape.643
  5.2 4.9 %all-to-all-start.1 = ((s32[32,1,544]{2,1,0:T(1,128)}), s32[32,1,544]{2,1,0:T(1,128)S(1)}, u32[]{:S(2)}, u32[]{:S(2)}) async-start(s32[32,1,544]{2,1,0:T(1,128)} %reshape.643), calls=%async_computation.1 | async-start | bytes 163840 | tf_op jit(solution)/shard_map/all_to_all | solution.py:170
  10.1 1.0 reshape.641
  12.0 4.6 %collective-permute-start.1 = (f32[3,1,5,128]{3,1,2,0:T(1,128)S(1)}, f32[3,1,5,128]{3,1,2,0:T(1,128)S(1)}, u32[]{:S(2)}, u32[]{:S(2)}) collective-permute-start(f32[3,1,5,128]{3,1,2,0:T(1,128)S(1)} %get-tuple-element.199), channel_id=1, source_target_pairs={{4,0},{8,4},{12,8},{16,12},{20,16},{24,20},{28,24},{0,28},{5,1},{9... | collective-permute-start | bytes 23048 | tf_op jit(solution)/shard_map/ppermute | solution.py:24
  16.6 0.8 broadcast_multiply_fusion.1
  18.1 0.8 broadcast_multiply_fusion
  18.9 2.4 collective-permute-done.2
  21.3 5.3 %copy.114 = f32[8,16384]{0,1:T(8,128)} copy(f32[8,16384]{1,0:T(8,128)S(1)} %copy-done.4) | data formatting | bytes 1048576 | tf_op args[1]
  26.6 0.9 copy.305
  29.7 6.4 %all-to-all-start = ((f32[32,3,544]{2,1,0:T(4,128)}), f32[32,3,544]{2,1,0:T(4,128)S(1)}, u32[]{:S(2)}, u32[]{:S(2)}) async-start(f32[32,3,544]{2,1,0:T(4,128)} %bitcast.259), calls=%async_computation | async-start | bytes 655360 | tf_op jit(solution)/shard_map/all_to_all | solution.py:172
  36.4 61.3 %gather_fusion = f32[17408,8]{1,0:T(8,128)} fusion(f32[16384,8]{1,0:T(8,128)} %bitcast.260, s32[17408]{0:T(1024)S(1)} %broadcast_clamp_fusion), kind=kCustom, calls=%fused_computation | custom fusion | bytes 1183744 | tf_op jit(solution)/shard_map/jit(_take)/gather | solution.py:138
  97.7 5.6 %copy.173 = f32[32,544,8]{1,0,2:T(8,128)S(1)} copy(f32[32,544,8]{2,1,0:T(8,128)} %bitcast.261) | data formatting | bytes 1114112 | tf_op jit(solution)/shard_map/jit(_take)/gather | solution.py:138
  104.4 5.8 %all-to-all-start.2 = ((f32[32,1,544]{2,1,0:T(1,128)}), f32[32,1,544]{2,1,0:T(1,128)S(1)}, u32[]{:S(2)}, u32[]{:S(2)}) async-start(f32[32,1,544]{2,1,0:T(1,128)} %copy.116), calls=%async_computation.2 | async-start | bytes 163840 | tf_op jit(solution)/shard_map/all_to_all | solution.py:143
  110.6 7.2 %all-to-all-done.2 = f32[32,1,544]{2,1,0:T(1,128)S(1)} async-done(((f32[32,1,544]{2,1,0:T(1,128)}), f32[32,1,544]{2,1,0:T(1,128)S(1)}, u32[]{:S(2)}, u32[]{:S(2)}) %all-to-all-start.2) | async-done | bytes 69664 | tf_op jit(solution)/shard_map/all_to_all | solution.py:143
  118.1 64.1 %scatter_custom_fusion = f32[6912]{0:T(1024)S(1)} fusion(s32[17408]{0:T(1024)S(1)} %bitcast.262, f32[17408]{0:T(1024)S(1)} %reshape.657, f32[]{:T(128)} %constant.313.clone.1), kind=kCustom, calls=%fused_computation.172 | custom fusion | bytes 27652 | tf_op jit(solution)/shard_map/scatter | solution.py:178
  185.8 5.7 %collective-permute-done.4 = f32[3,1,5,128]{3,1,2,0:T(1,128)S(1)} collective-permute-done((f32[3,1,5,128]{3,1,2,0:T(1,128)S(1)}, f32[3,1,5,128]{3,1,2,0:T(1,128)S(1)}, u32[]{:S(2)}, u32[]{:S(2)}) %collective-permute-start.4) | collective-permute-done | bytes 7712 | tf_op jit(solution)/shard_map/ppermute | solution.py:21
  191.6 3.6 %collective-permute-done.5 = f32[3,1,5,128]{3,1,2,0:T(1,128)S(1)} collective-permute-done((f32[3,1,5,128]{3,1,2,0:T(1,128)S(1)}, f32[3,1,5,128]{3,1,2,0:T(1,128)S(1)}, u32[]{:S(2)}, u32[]{:S(2)}) %collective-permute-start.5) | collective-permute-done | bytes 7712 | tf_op jit(solution)/shard_map/ppermute | solution.py:24
  195.3 3.1 collective-permute-done.6
  198.5 1.4 collective-permute-done.7
  203.0 0.8 fusion.43
  206.3 2.0 stack.121
  208.3 37.2 %psum.14 = f32[6]{0:T(128)S(1)} all-reduce(f32[6]{0:T(128)S(1)} %stack.121), channel_id=1, replica_groups=mesh['mesh'=8,'bg'=4] {'mesh','bg'}, use_global_device_ids=true, to_apply=%region_18.19 | all-reduce | flops 6 | bytes 48 | tf_op jit(solution)/shard_map/psum | solution.py:192
  261.5 2.3 collective-permute-start.8
  263.9 4.1 %collective-permute-done.8 = f32[3,1,5,128]{3,1,2,0:T(1,128)S(1)} collective-permute-done((f32[3,1,5,128]{3,1,2,0:T(1,128)S(1)}, f32[3,1,5,128]{3,1,2,0:T(1,128)S(1)}, u32[]{:S(2)}, u32[]{:S(2)}) %collective-permute-start.8) | collective-permute-done | bytes 7712 | tf_op jit(solution)/shard_map/ppermute | solution.py:21
  267.9 1.3 collective-permute-start.9
  269.3 2.4 collective-permute-done.9
  271.8 3.1 collective-permute-done.10
  274.9 1.4 collective-permute-done.11
  279.4 0.8 fusion.49
  282.8 2.0 stack.136
  284.7 40.0 %psum.15 = f32[6]{0:T(128)S(1)} all-reduce(f32[6]{0:T(128)S(1)} %stack.136), channel_id=1, replica_groups=mesh['mesh'=8,'bg'=4] {'mesh','bg'}, use_global_device_ids=true, to_apply=%region_36.37 | all-reduce | flops 6 | bytes 48 | tf_op jit(solution)/shard_map/psum | solution.py:192
  (135 shorter events, 23.4 us)
Async XLA Ops:
  0.6 20.6 %copy-start.4 = (f32[8,16384]{1,0:T(8,128)S(1)}, f32[8,16384]{1,0:T(8,128)}, u32[]{:S(2)}) copy-start(f32[8,16384]{1,0:T(8,128)} %param.39) | copy-start | bytes 1572868
  0.7 11.4 %collective-permute-start = (f32[3,1,5,128]{3,1,2,0:T(1,128)S(1)}, f32[3,1,5,128]{3,1,2,0:T(1,128)S(1)}, u32[]{:S(2)}, u32[]{:S(2)}) collective-permute-start(f32[3,1,5,128]{3,1,2,0:T(1,128)S(1)} %slice.391), channel_id=1, source_target_pairs={{0,4},{4,8},{8,12},{12,16},{16,20},{20,24},{24,28},{28,0},{1,5},{5... | collective-permute-start | bytes 23048 | tf_op jit(solution)/shard_map/ppermute | solution.py:21
  5.2 24.4 %all-to-all-start.1 = ((s32[32,1,544]{2,1,0:T(1,128)}), s32[32,1,544]{2,1,0:T(1,128)S(1)}, u32[]{:S(2)}, u32[]{:S(2)}) async-start(s32[32,1,544]{2,1,0:T(1,128)} %reshape.643), calls=%async_computation.1 | async-start | bytes 163840 | tf_op jit(solution)/shard_map/all_to_all | solution.py:170
  12.0 6.0 %collective-permute-start.1 = (f32[3,1,5,128]{3,1,2,0:T(1,128)S(1)}, f32[3,1,5,128]{3,1,2,0:T(1,128)S(1)}, u32[]{:S(2)}, u32[]{:S(2)}) collective-permute-start(f32[3,1,5,128]{3,1,2,0:T(1,128)S(1)} %get-tuple-element.199), channel_id=1, source_target_pairs={{4,0},{8,4},{12,8},{16,12},{20,16},{24,20},{28,24},{0,28},{5,1},{9... | collective-permute-start | bytes 23048 | tf_op jit(solution)/shard_map/ppermute | solution.py:24
  18.1 3.2 collective-permute-start.2
  21.2 6.2 %collective-permute-start.3 = (f32[3,5,1,128]{3,1,2,0:T(8,128)S(1)}, f32[3,5,1,128]{3,1,2,0:T(8,128)S(1)}, u32[]{:S(2)}, u32[]{:S(2)}) collective-permute-start(f32[3,5,1,128]{3,1,2,0:T(8,128)S(1)} %get-tuple-element.197), channel_id=1, source_target_pairs={{1,0},{2,1},{3,2},{0,3},{5,4},{6,5},{7,6},{4,7},{9,8},{10,9},{11,1... | collective-permute-start | bytes 23048 | tf_op jit(solution)/shard_map/ppermute | solution.py:24
  21.3 5.3 %copy-start.5 = (f32[1,32,3,544]{3,1,2,0:T(8,128)S(1)}, f32[1,32,3,544]{3,1,2,0:T(8,128)}, u32[]{:S(2)}) copy-start(f32[1,32,3,544]{3,1,2,0:T(8,128)} %param.42) | copy-start | bytes 626692
  21.3 6.2 %copy-start.3 = (f32[5,6,1,1]{0,1,3,2:T(8,128)S(1)}, f32[5,6,1,1]{0,1,3,2:T(8,128)}, u32[]{:S(2)}) copy-start(f32[5,6,1,1]{0,1,3,2:T(8,128)} %constant.344) | copy-start | bytes 364
  21.3 6.4 %copy-start.2 = (f32[5,6,1,1]{0,1,3,2:T(8,128)S(1)}, f32[5,6,1,1]{0,1,3,2:T(8,128)}, u32[]{:S(2)}) copy-start(f32[5,6,1,1]{0,1,3,2:T(8,128)} %constant.342) | copy-start | bytes 364
  26.6 1.9 copy-start
  26.6 2.6 copy-start.1
  29.7 73.7 %all-to-all-start = ((f32[32,3,544]{2,1,0:T(4,128)}), f32[32,3,544]{2,1,0:T(4,128)S(1)}, u32[]{:S(2)}, u32[]{:S(2)}) async-start(f32[32,3,544]{2,1,0:T(4,128)} %bitcast.259), calls=%async_computation | async-start | bytes 655360 | tf_op jit(solution)/shard_map/all_to_all | solution.py:172
  104.4 13.4 %all-to-all-start.2 = ((f32[32,1,544]{2,1,0:T(1,128)}), f32[32,1,544]{2,1,0:T(1,128)S(1)}, u32[]{:S(2)}, u32[]{:S(2)}) async-start(f32[32,1,544]{2,1,0:T(1,128)} %copy.116), calls=%async_computation.2 | async-start | bytes 163840 | tf_op jit(solution)/shard_map/all_to_all | solution.py:143
  185.1 6.4 %collective-permute-start.4 = (f32[3,1,5,128]{3,1,2,0:T(1,128)S(1)}, f32[3,1,5,128]{3,1,2,0:T(1,128)S(1)}, u32[]{:S(2)}, u32[]{:S(2)}) collective-permute-start(f32[3,1,5,128]{3,1,2,0:T(1,128)S(1)} %slice.440), channel_id=1, source_target_pairs={{0,4},{4,8},{8,12},{12,16},{16,20},{20,24},{24,28},{28,0},{1,5},{5... | collective-permute-start | bytes 23048 | tf_op jit(solution)/shard_map/ppermute | solution.py:21
  191.5 3.7 %collective-permute-start.5 = (f32[3,1,5,128]{3,1,2,0:T(1,128)S(1)}, f32[3,1,5,128]{3,1,2,0:T(1,128)S(1)}, u32[]{:S(2)}, u32[]{:S(2)}) collective-permute-start(f32[3,1,5,128]{3,1,2,0:T(1,128)S(1)} %get-tuple-element.195), channel_id=1, source_target_pairs={{4,0},{8,4},{12,8},{16,12},{20,16},{24,20},{28,24},{0,28},{5,1},{9... | collective-permute-start | bytes 23048 | tf_op jit(solution)/shard_map/ppermute | solution.py:24
  195.3 3.2 collective-permute-start.6
  198.5 1.4 collective-permute-start.7
  201.9 1.1 copy-start.6
  261.5 6.4 %collective-permute-start.8 = (f32[3,1,5,128]{3,1,2,0:T(1,128)S(1)}, f32[3,1,5,128]{3,1,2,0:T(1,128)S(1)}, u32[]{:S(2)}, u32[]{:S(2)}) collective-permute-start(f32[3,1,5,128]{3,1,2,0:T(1,128)S(1)} %slice.446), channel_id=1, source_target_pairs={{0,4},{4,8},{8,12},{12,16},{16,20},{20,24},{24,28},{28,0},{1,5},{5... | collective-permute-start | bytes 23048 | tf_op jit(solution)/shard_map/ppermute | solution.py:21
  267.9 3.7 %collective-permute-start.9 = (f32[3,1,5,128]{3,1,2,0:T(1,128)S(1)}, f32[3,1,5,128]{3,1,2,0:T(1,128)S(1)}, u32[]{:S(2)}, u32[]{:S(2)}) collective-permute-start(f32[3,1,5,128]{3,1,2,0:T(1,128)S(1)} %get-tuple-element.191), channel_id=1, source_target_pairs={{4,0},{8,4},{12,8},{16,12},{20,16},{24,20},{28,24},{0,28},{5,1},{9... | collective-permute-start | bytes 23048 | tf_op jit(solution)/shard_map/ppermute | solution.py:24
  271.7 3.2 collective-permute-start.10
  274.9 1.4 collective-permute-start.11
where the time goes:
time: 338 us; the launch traced here: 337 us
  local copies, waits for them, and re-layouts  148 us (44%)
  blocking collectives  77.2 us (23%)
  waiting for transfers between devices  34.8 us (10%)
  starting transfers between devices  29.2 us (9%)
  between operations  26.6 us (8%)
  matrix products  12.1 us (4%)
  other arithmetic  8.78 us (3%)
    psum x2, blocking collectives, shards(): totals = lax.psum(partial_terms, ('mesh', 'bg'))  77.2 us
    gather x2, local copies, waits for them, and re-layouts, gather_coefs(): corner_rows = jnp.take(jnp.transpose(table), index_rows, axis=0)  66.8 us
    scatter x1, local copies, waits for them, and re-layouts, shards(): target_size_scale = jnp.zeros((point_count,), jnp.float32).at[query_point...  64.1 us
    ppermute x6, waiting for transfers between devices, extended(): lax.ppermute(lax.slice_in_dim(block, block.shape[dim] - width, None, axis...  18.3 us
    ppermute x6, waiting for transfers between devices, extended(): lax.ppermute(lax.slice_in_dim(block, 0, width, axis=dim), axis, backward)  9.26 us
    unnamed x18, local copies, waits for them, and re-layouts  7.56 us
    all_to_all x1, waiting for transfers between devices, answer(): lax.all_to_all(reply, ('mesh', 'bg'), split_axis=0, concat_axis=0, tiled=...  7.21 us
  transfers between devices with their start and end apart: 15, of which 11 were waited for; matrix products, arithmetic and copies ran while one was open for 24% of the time, Pallas kernels for 0%

commit v1 on v0

v1 whole, which is shorter than its diff:
```python
import functools

import jax
import jax.numpy as jnp
import numpy as np
from jax import lax
from jax.experimental import pallas as pl
from jax.experimental.pallas import tpu as pltpu
from jax.sharding import PartitionSpec as P

PASSES = 2
LS_STEPS = 4
ROW = 8
LO = 256

GAUSS_POINTS = np.array([0.5 - 0.5 * np.sqrt(0.6), 0.5, 0.5 + 0.5 * np.sqrt(0.6)])
GAUSS_WEIGHTS = np.array([5.0 / 18.0, 8.0 / 18.0, 5.0 / 18.0])
MESH = pl.DeviceIdType.MESH
HIGHEST = lax.Precision.HIGHEST


def basis_tables(elements, periodic):
    node_count = 2 * elements if periodic else 2 * elements + 1
    values = np.zeros((node_count, 3 * elements))
    slopes = np.zeros((node_count, 3 * elements))
    points = GAUSS_POINTS
    shape_values = [
        2.0 * (points - 0.5) * (points - 1.0),
        -4.0 * points * (points - 1.0),
        2.0 * points * (points - 0.5),
    ]
    shape_slopes = [4.0 * points - 3.0, 4.0 - 8.0 * points, 4.0 * points - 1.0]
    for offset in range(3):
        node_rows = (2 * np.arange(elements) + offset) % node_count
        for gauss_index in range(3):
            columns = 3 * np.arange(elements) + gauss_index
            values[node_rows, columns] += shape_values[offset][gauss_index]
            slopes[node_rows, columns] += shape_slopes[offset][gauss_index]
    return values, slopes


def round_up(value, unit):
    return -(-value // unit) * unit


def make_tables(ze, ye, xe):
    zv, zs = basis_tables(ze, False)
    yv, ys = basis_tables(ye, False)
    xv, xs = basis_tables(xe, True)
    nz, ny = zv.shape[0], yv.shape[0]
    qr, qx = 9 * ze * ye, 3 * xe
    qrp, qxp = round_up(qr, 8), round_up(qx, 128)

    def rows(tz, ty):
        out = np.zeros((qrp, nz, ROW))
        out[:qr, :, :ny] = np.einsum("zk,yl->klzy", tz, ty).reshape(qr, nz, ny)
        return out.reshape(qrp, nz * ROW)

    vv, vd, dv = rows(zv, yv), rows(zv, ys), rows(zs, yv)
    along_x = np.zeros((2 * xe, 2 * qxp))
    along_x[:, :qx] = xv
    along_x[:, qxp : qxp + qx] = xs
    weights = np.zeros((qrp, qxp))
    weights[:qr, :qx] = np.einsum(
        "z,y,x->zyx",
        np.tile(GAUSS_WEIGHTS, ze),
        np.tile(GAUSS_WEIGHTS, ye),
        np.tile(GAUSS_WEIGHTS, xe),
    ).reshape(qr, qx)
    tables = (
        along_x,
        along_x.T,
        vv,
        np.concatenate([vd, dv], axis=0),
        vv.T,
        np.concatenate([vd.T, dv.T], axis=1),
        weights,
    )
    return tuple(np.ascontiguousarray(t).astype(np.float32) for t in tables)


def dot(a, b):
    return lax.dot_general(
        a, b, (((1,), (0,)), ((), ())), precision=HIGHEST, preferred_element_type=jnp.float32
    )


def kernel(
    dims,
    disp, coef, elem, point, coord, xt, xtt, vv, vdv, vvt, vdvt, wts,
    out, lc,
    query, arrived, answer, found, tab32, tab, scat, fld, grad,
    hy_send, hc_send, hz, hy, hc,
    ysend, csend, zrecv, yrecv, crecv, part, sums,
    q_send, q_recv, f_send, f_recv, h_send, h_recv, x_send, x_recv, a_send, a_recv,
):
    n_mesh, n_bg, nz, ny, qx = dims
    n = n_mesh * n_bg
    cap = elem.shape[1]
    his = coef.shape[1] // LO
    qrp, qxp = wts.shape
    zi, yi = lax.axis_index("mesh"), lax.axis_index("bg")
    me = zi * n_bg + yi

    def device(index):
        return (lax.div(index, n_bg), lax.rem(index, n_bg))

    def near(dz, dy):
        return (lax.rem(zi + n_mesh + dz, n_mesh), lax.rem(yi + n_bg + dy, n_bg))

    def remote(src, dst, ssem, rsem, target):
        return pltpu.make_async_remote_copy(
            src_ref=src, dst_ref=dst, send_sem=ssem, recv_sem=rsem,
            device_id=target, device_id_type=MESH,
        )

    def wait_bytes(ref, sem):
        pltpu.make_async_copy(ref, ref, sem).wait()

    barrier = pltpu.get_barrier_semaphore()

    def greet(d, carry):
        pl.semaphore_signal(
            barrier, inc=1, device_id=device(lax.rem(me + d, n)), device_id_type=MESH
        )
        return carry

    lax.fori_loop(1, n, greet, 0)

    def pack(o, carry):
        query[o, 0:1, :] = elem[pl.ds(o, 1), :].astype(jnp.float32)
        query[o, 1:4, :] = coord[o]
        return carry

    lax.fori_loop(0, n, pack, 0)
    for c in range(3):
        for z in range(nz - 1):
            hy_send[c, z : z + 1, :] = disp[c, z, 0:1, :]
        hc_send[c : c + 1, :] = disp[c, 0, 0:1, :]
    pl.semaphore_wait(barrier, n - 1)

    def send_query(d, carry):
        target = lax.rem(me + d, n)
        remote(
            query.at[target], arrived.at[d], q_send, q_recv.at[d], device(target)
        ).start()
        return carry

    lax.fori_loop(1, n, send_query, 0)
    halo = [
        remote(disp.at[:, 0], hz, h_send.at[0], h_recv.at[0], near(-1, 0)),
        remote(hy_send, hy, h_send.at[1], h_recv.at[1], near(0, -1)),
        remote(hc_send, hc, h_send.at[2], h_recv.at[2], near(-1, -1)),
    ]
    for copy in halo:
        copy.start()

    for h in range(his):
        tab32[8 * h : 8 * h + 8, :] = coef[:, LO * h : LO * h + LO]
    whole = tab32[...]
    top = whole.astype(jnp.bfloat16)
    tab[:, :LO] = top
    tab[:, LO:] = (whole - top.astype(jnp.float32)).astype(jnp.bfloat16)
    arrived[0] = query[me]

    corner = lax.broadcasted_iota(jnp.int32, (8, cap), 0)
    lo_rows = lax.broadcasted_iota(jnp.int32, (LO, cap), 0)

    def serve(d):
        ids = arrived[d, 0:1, :].astype(jnp.int32)
        hi = lax.shift_right_logical(ids, LO.bit_length() - 1)
        lo = lax.bitwise_and(ids, LO - 1)
        one_hot = jnp.where(lo_rows == lo, 1.0, 0.0).astype(jnp.bfloat16)
        one_hot = jnp.concatenate([one_hot, one_hot], axis=0)
        rows = lax.dot_general(
            tab[...], one_hot, (((1,), (0,)), ((), ())), preferred_element_type=jnp.float32
        )
        hi8 = jnp.broadcast_to(hi, (8, cap))
        chosen = rows[0:8]
        for h in range(1, his):
            chosen = jnp.where(hi8 == h, rows[8 * h : 8 * h + 8], chosen)
        x, y, z = (arrived[d, j : j + 1, :] for j in (1, 2, 3))
        ax = jnp.where((corner & 1) != 0, x, 1.0 - x)
        ay = jnp.where((corner & 2) != 0, y, 1.0 - y)
        az = jnp.where((corner & 4) != 0, z, 1.0 - z)
        lsize = jnp.sum(ax * ay * az * chosen, axis=0, keepdims=True)
        return jnp.exp(-2.0 * lsize)

    found[me] = serve(0)

    def serve_remote(d, carry):
        source = lax.rem(me + n - d, n)
        remote(query.at[0], arrived.at[d], q_send, q_recv.at[d], device(source)).wait_recv()
        answer[d] = serve(d)
        remote(answer.at[d], found.at[me], f_send, f_recv, device(source)).start()
        return carry

    lax.fori_loop(1, n, serve_remote, 0)

    for copy in halo:
        copy.wait()
    fld[...] = jnp.zeros_like(fld)
    for c in range(3):
        for z in range(nz - 1):
            fld[c, z, 0 : ny - 1, :] = disp[c, z]
            fld[c, z, ny - 1 : ny, :] = hy[c, z : z + 1, :]
        fld[c, nz - 1, 0 : ny - 1, :] = hz[c]
        fld[c, nz - 1, ny - 1 : ny, :] = hc[c : c + 1, :]

    def derivatives(flat):
        along = dot(flat, xt[...])
        result = []
        for c in range(3):
            rows = along[c * nz * ROW : (c + 1) * nz * ROW]
            dx = dot(vv[...], rows[:, qxp:])
            dyz = dot(vdv[...], rows[:, :qxp])
            result.append([dx, dyz[:qrp], dyz[qrp:]])
        return result

    jac = derivatives(fld[...].reshape(3 * nz * ROW, -1))
    for c in range(3):
        jac[c][c] = jac[c][c] + 1.0

    wait_bytes(found.at[pl.ds(0, n - 1)], f_recv)
    scat[...] = jnp.zeros_like(scat)
    hi_rows = lax.broadcasted_iota(jnp.int32, (qrp, cap), 0)
    qx_rows = lax.broadcasted_iota(jnp.int32, (qxp, cap), 0)

    def place(o, carry):
        p = point[pl.ds(o, 1), :].astype(jnp.float32)
        hi = jnp.floor((p + 0.5) * (1.0 / qx))
        lo = (p - hi * qx).astype(jnp.int32)
        mine = hi_rows == hi.astype(jnp.int32)
        value = found[o]
        pieces = []
        for _ in range(3):
            piece = value.astype(jnp.bfloat16).astype(jnp.float32)
            value = value - piece
            pieces.append(jnp.where(mine, piece, 0.0).astype(jnp.bfloat16))
        left = jnp.concatenate(pieces, axis=0)
        right = jnp.where(qx_rows == lo, 1.0, 0.0).astype(jnp.bfloat16)
        scat[...] += lax.dot_general(
            left, right, (((1,), (1,)), ((), ())), preferred_element_type=jnp.float32
        )
        return carry

    lax.fori_loop(0, n, place, 0)
    scale = scat[:qrp] + scat[qrp : 2 * qrp] + scat[2 * qrp :]
    weights = wts[...]
    scale = jnp.where(weights > 0.0, scale, 0.0)

    pairs = [(k, l) for k in range(3) for l in range(k, 3)]

    def gram(a, b):
        return {
            (k, l): a[0][k] * b[0][l] + a[1][k] * b[1][l] + a[2][k] * b[2][l]
            for k, l in (pairs if a is b else [(k, l) for k in range(3) for l in range(3)])
        }

    def inner(a, b):
        diag = sum(a[k, k] * b[k, k] for k in range(3))
        off = a[0, 1] * b[0, 1] + a[0, 2] * b[0, 2] + a[1, 2] * b[1, 2]
        return jnp.sum(weights * (diag + 2.0 * off), axis=0, keepdims=True)

    for turn in range(PASSES):
        gr = gram(jac, jac)
        r0 = {kl: gr[kl] * scale - (1.0 if kl[0] == kl[1] else 0.0) for kl in pairs}
        factor = (4.0 * weights) * scale
        for c in range(3):
            pulled = []
            for k in range(3):
                total = sum(r0[min(k, l), max(k, l)] * jac[c][l] for l in range(3))
                pulled.append(total * factor)
            by_value = dot(vdvt[...], jnp.concatenate([pulled[1], pulled[2]], axis=0))
            by_slope = dot(vvt[...], pulled[0])
            node = dot(jnp.concatenate([by_value, by_slope], axis=1), xtt[...])
            grad[turn, c] = node.reshape(nz, ROW, -1)

        for c in range(3):
            for side, y in enumerate((0, ny - 1)):
                for z in range(nz):
                    ysend[turn, side, c, z : z + 1, :] = grad[turn, c, z, y : y + 1, :]
                for zside, z in enumerate((0, nz - 1)):
                    csend[turn, 2 * zside + side, c : c + 1, :] = grad[turn, c, z, y : y + 1, :]
        copies = []
        for side, step in enumerate((-1, 1)):
            plane = (0, nz - 1)[side]
            copies.append((grad.at[turn, :, plane], zrecv.at[turn, 1 - side], near(step, 0)))
            copies.append((ysend.at[turn, side], yrecv.at[turn, 1 - side], near(0, step)))
            for other, ystep in enumerate((-1, 1)):
                index = 2 * side + other
                copies.append((csend.at[turn, index], crecv.at[turn, 3 - index], near(step, ystep)))
        copies = [
            remote(src, dst, x_send.at[8 * turn + i], x_recv.at[8 * turn + i], target)
            for i, (src, dst, target) in enumerate(copies)
        ]
        for copy in copies:
            copy.start()
        for copy in copies:
            copy.wait()
        for c in range(3):
            for side, z in enumerate((0, nz - 1)):
                grad[turn, c, z] += zrecv[turn, side, c]
            for side, y in enumerate((0, ny - 1)):
                for z in range(nz):
                    grad[turn, c, z, y : y + 1, :] += yrecv[turn, side, c, z : z + 1, :]
                for zside, z in enumerate((0, nz - 1)):
                    grad[turn, c, z, y : y + 1, :] += crecv[turn, 2 * zside + side, c : c + 1, :]

        direction = -grad[turn]
        move = derivatives(direction.reshape(3 * nz * ROW, -1))
        mixed = gram(jac, move)
        r1 = {(k, l): (mixed[k, l] + mixed[l, k]) * scale for k, l in pairs}
        mm = gram(move, move)
        r2 = {kl: mm[kl] * scale for kl in pairs}
        terms = [
            inner(r0, r0), inner(r0, r1), inner(r0, r2),
            inner(r1, r2), inner(r2, r2), inner(r1, r1),
        ]
        terms = jnp.concatenate(terms + [jnp.zeros((2, qxp), jnp.float32)], axis=0)
        mine = terms[:, :128]
        for lane in range(128, qxp, 128):
            mine = mine + terms[:, lane : lane + 128]
        part[turn] = mine
        sums[turn, me] = mine

        def share(d, carry, turn=turn):
            remote(
                part.at[turn], sums.at[turn, me], a_send.at[turn], a_recv.at[turn],
                device(lax.rem(me + d, n)),
            ).start()
            return carry

        lax.fori_loop(1, n, share, 0)
        wait_bytes(sums.at[turn, pl.ds(0, n - 1)], a_recv.at[turn])
        totals = jnp.sum(jnp.sum(sums[turn], axis=0), axis=1, keepdims=True)
        d00, d01, d02, d12, d22, gn = (
            jnp.broadcast_to(totals[i : i + 1], (1, 128)) for i in range(6)
        )
        c0, c1, c2, c3, c4 = d00, 2.0 * d01, gn + 2.0 * d02, 2.0 * d12, d22
        t = jnp.zeros((1, 128), jnp.float32)
        for _ in range(LS_STEPS):
            slope = c1 + t * (2.0 * c2 + t * (3.0 * c3 + t * 4.0 * c4))
            curvature = 2.0 * c2 + t * (6.0 * c3 + t * 12.0 * c4)
            t = t - slope / jnp.maximum(curvature, gn + 1e-06)
        count = n * (qrp // 9) * (qx // 3)
        for i, value in enumerate((c0, c1, c2, c3, c4)):
            lc[turn : turn + 1, i : i + 1] = value[:, :1] / count
        fld[...] = fld[...] + t.reshape(1, 1, 1, 128) * direction
        if turn + 1 < PASSES:
            wide = t[:, :1]
            jac = [[jac[c][k] + wide * move[c][k] for k in range(3)] for c in range(3)]

    for c in range(3):
        for z in range(nz - 1):
            out[c, z] = fld[c, z, 0 : ny - 1, :]

    wait_bytes(query.at[pl.ds(0, n - 1)], q_send)
    wait_bytes(answer.at[pl.ds(0, n - 1)], f_send)
    for turn in range(PASSES):
        wait_bytes(sums.at[turn, pl.ds(0, n - 1)], a_send.at[turn])


def shards(mesh_shape, displacement, bg_coef, query_elem, query_point, query_coord):
    n_mesh, n_bg = mesh_shape
    n = n_mesh * n_bg
    _, nz0, ny0, nx = displacement.shape
    ze, ye, xe = nz0 // 2, ny0 // 2, nx // 2
    nz, ny = nz0 + 1, ny0 + 1
    assert ny <= ROW and nx == 128
    cap = query_elem.shape[2]
    tables = make_tables(ze, ye, xe)
    qrp, qxp = tables[-1].shape
    his = bg_coef.shape[1] // LO
    f32 = jnp.float32
    dims = (n_mesh, n_bg, nz, ny, 3 * xe)
    vmem = pl.BlockSpec(memory_space=pltpu.VMEM)
    dma = pltpu.SemaphoreType.DMA
    scratch = [
        pltpu.VMEM((n, 4, cap), f32),
        pltpu.VMEM((n, 4, cap), f32),
        pltpu.VMEM((n, 1, cap), f32),
        pltpu.VMEM((n, 1, cap), f32),
        pltpu.VMEM((8 * his, LO), f32),
        pltpu.VMEM((8 * his, 2 * LO), jnp.bfloat16),
        pltpu.VMEM((3 * qrp, qxp), f32),
        pltpu.VMEM((3, nz, ROW, nx), f32),
        pltpu.VMEM((PASSES, 3, nz, ROW, nx), f32),
        pltpu.VMEM((3, nz0, nx), f32),
        pltpu.VMEM((3, nx), f32),
        pltpu.VMEM((3, ny0, nx), f32),
        pltpu.VMEM((3, nz0, nx), f32),
        pltpu.VMEM((3, nx), f32),
        pltpu.VMEM((PASSES, 2, 3, nz, nx), f32),
        pltpu.VMEM((PASSES, 4, 3, nx), f32),
        pltpu.VMEM((PASSES, 2, 3, ROW, nx), f32),
        pltpu.VMEM((PASSES, 2, 3, nz, nx), f32),
        pltpu.VMEM((PASSES, 4, 3, nx), f32),
        pltpu.VMEM((PASSES, 8, 128), f32),
        pltpu.VMEM((PASSES, n, 8, 128), f32),
        dma, dma((n,)), dma, dma, dma((3,)), dma((3,)),
        dma((8 * PASSES,)), dma((8 * PASSES,)), dma((PASSES,)), dma((PASSES,)),
    ]
    out, lc = pl.pallas_call(
        functools.partial(kernel, dims),
        out_shape=(
            jax.ShapeDtypeStruct(displacement.shape, f32),
            jax.ShapeDtypeStruct((PASSES, 5), f32),
        ),
        in_specs=[vmem] * 12,
        out_specs=(vmem, vmem),
        scratch_shapes=scratch,
        compiler_params=pltpu.CompilerParams(
            collective_id=0, has_side_effects=True, vmem_limit_bytes=48 * 2**20
        ),
    )(
        displacement, bg_coef, query_elem[0], query_point[0], query_coord[0],
        *(jnp.asarray(t) for t in tables),
    )
    return out, lc


def solution(mesh):
    in_specs = (
        P(None, "mesh", "bg", None),
        P(None, ("mesh", "bg")),
        P(("mesh", "bg"), None, None),
        P(("mesh", "bg"), None, None),
        P(("mesh", "bg"), None, None, None),
    )
    out_specs = (P(None, "mesh", "bg", None), P())
    body = functools.partial(shards, (mesh.shape["mesh"], mesh.shape["bg"]))
    return jax.shard_map(body, mesh=mesh, in_specs=in_specs, out_specs=out_specs, check_vma=False)
```

time: 338 us -> 72.3 us (0.21)
  local copies, waits for them, and re-layouts: 148 us -> 9.72 us
  blocking collectives: 77.2 us -> 0 us
  Pallas kernels: 0 us -> 61.3 us
  waiting for transfers between devices: 34.8 us -> 0 us
  starting transfers between devices: 29.2 us -> 0 us
  between operations: 26.6 us -> 0.69 us
  matrix products: 12.1 us -> 0 us
  other arithmetic: 8.78 us -> 0 us
    psum x2 -> x0, blocking collectives: 77.2 us -> none  [shards(): totals = lax.psum(partial_terms, ('mesh', 'bg'))]
    gather x2 -> x0, local copies, waits for them, and re-layouts: 66.8 us -> none  [gather_coefs(): corner_rows = jnp.take(jnp.transpose(table), index_rows, axis=0)]
    scatter x1 -> x0, local copies, waits for them, and re-layouts: 64.1 us -> none  [shards(): target_size_scale = jnp.zeros((point_count,), jnp.float32).at[query_point...]
    pallas_call x0 -> x1, Pallas kernels: none -> 61.3 us  [shards(): pl.pallas_call(functools.partial(kernel, dims), out_shape=(jax.ShapeDtype...]
    ppermute x12 -> x0, waiting for transfers between devices: 27.6 us -> none  [the longest x6 18.3 us: extended(): lax.ppermute(lax.slice_in_dim(block, block.shape[dim] - width, None, axis...]
    all_to_all x3 -> x0, starting transfers between devices: 17.1 us -> none  [the longest x1 6.37 us: shards(): lax.all_to_all(coords, ('mesh', 'bg'), split_axis=0, concat_axis=0, tiled...]
    dot_general x48 -> x0, matrix products: 12.1 us -> none  [the longest x6 1.92 us: gradients(): jnp.einsum('cklx,xm->cklm', slope_zy, value_along_x, precision=highest)]
    ppermute x12 -> x0, starting transfers between devices: 12.1 us -> none  [the longest x6 6.17 us: extended(): lax.ppermute(lax.slice_in_dim(block, block.shape[dim] - width, None, axis...]
  transfers between devices with their start and end apart: 15 -> 0, of which waited for: 11 -> 0; matrix products, arithmetic and copies ran while one was open for 24% -> 0% of each run, Pallas kernels for 0% -> 0%
where the time goes in v1:
time: 72.3 us; the launch traced here: 71.7 us
  Pallas kernels  61.3 us (85%)
  local copies, waits for them, and re-layouts  9.72 us (13%)
    pallas_call x1, Pallas kernels, shards(): pl.pallas_call(functools.partial(kernel, dims), out_shape=(jax.ShapeDtype...  61.3 us
    unnamed x25, local copies, waits for them, and re-layouts  9.72 us

profile of v1, /device:TPU:0, one launch (start us, length us, event | category | flops | bytes accessed | tf_op | source)
XLA Modules:
  0.0 71.7 jit_solution(9275515238085353869)
XLA Ops:
  0.6 0.0 copy-start
  0.6 0.0 copy-start.5
  0.7 1.2 %copy.16 = f32[1,32,3,544]{3,2,1,0:T(4,128)S(1)} copy(f32[1,32,3,544]{3,1,2,0:T(8,128)} %param.16) | data formatting | bytes 417792 | tf_op args[4]
  1.8 0.0 copy-done
  1.8 0.0 copy-done.5
  1.8 0.0 copy-start.1
  1.9 0.9 %copy-done.1 = f32[512,128]{1,0:T(8,128)S(1)} copy-done((f32[512,128]{1,0:T(8,128)S(1)}, f32[512,128]{1,0:T(8,128)}, u32[]{:S(2)}) %copy-start.1) | copy-done | bytes 262168
  2.8 0.0 copy-start.2
  2.8 0.9 %copy-done.2 = f32[128,512]{1,0:T(8,128)S(1)} copy-done((f32[128,512]{1,0:T(8,128)S(1)}, f32[128,512]{1,0:T(8,128)}, u32[]{:S(2)}) %copy-start.2) | copy-done | bytes 262168
  3.8 0.0 copy-start.3
  3.8 0.9 %copy-done.3 = s32[1,32,544]{2,1,0:T(8,128)S(1)} copy-done((s32[1,32,544]{2,1,0:T(8,128)S(1)}, s32[1,32,544]{2,1,0:T(8,128)}, u32[]{:S(2)}) %copy-start.3) | copy-done | bytes 69656
  4.6 0.0 copy-start.4
  4.6 0.9 %copy-done.4 = s32[1,32,544]{2,1,0:T(8,128)S(1)} copy-done((s32[1,32,544]{2,1,0:T(8,128)S(1)}, s32[1,32,544]{2,1,0:T(8,128)}, u32[]{:S(2)}) %copy-start.4) | copy-done | bytes 69656
  5.5 0.0 copy-start.6
  5.5 0.8 %copy-done.6 = f32[80,40]{1,0:T(8,128)S(1)} copy-done((f32[80,40]{1,0:T(8,128)S(1)}, f32[80,40]{1,0:T(8,128)}, u32[]{:S(2)}) %copy-start.6) | copy-done | bytes 12824
  6.3 0.0 copy-start.7
  6.3 0.7 %copy-done.7 = f32[3,4,4,128]{3,2,1,0:T(4,128)S(1)} copy-done((f32[3,4,4,128]{3,2,1,0:T(4,128)S(1)}, f32[3,4,4,128]{3,2,1,0:T(4,128)}, u32[]{:S(2)}) %copy-start.7) | copy-done | bytes 24600
  7.0 0.0 copy-start.8
  7.0 0.7 %copy-done.8 = f32[40,80]{1,0:T(8,128)S(1)} copy-done((f32[40,80]{1,0:T(8,128)S(1)}, f32[40,80]{1,0:T(8,128)}, u32[]{:S(2)}) %copy-start.8) | copy-done | bytes 12824
  7.8 0.0 copy-start.9
  7.8 0.7 %copy-done.9 = f32[40,40]{1,0:T(8,128)S(1)} copy-done((f32[40,40]{1,0:T(8,128)S(1)}, f32[40,40]{1,0:T(8,128)}, u32[]{:S(2)}) %copy-start.9) | copy-done | bytes 6424
  8.5 0.0 copy-start.10
  8.5 0.7 %copy-done.10 = f32[40,40]{1,0:T(8,128)S(1)} copy-done((f32[40,40]{1,0:T(8,128)S(1)}, f32[40,40]{1,0:T(8,128)}, u32[]{:S(2)}) %copy-start.10) | copy-done | bytes 6424
  9.2 61.3 %shard_map.131 = (f32[3,4,4,128]{3,2,1,0:T(4,128)S(1)}, f32[2,5]{1,0:T(2,128)S(1)}) custom-call(f32[3,4,4,128]{3,2,1,0:T(4,128)S(1)} %copy-done.7, f32[8,16384]{1,0:T(8,128)S(1)} %copy-done, s32[32,544]{1,0:T(8,128)S(1)} %bitcast.6, s32[32,544]{1,0:T(8,128)S(1)} %bitcast.7, f32[32,3,544]{2,1,0:T(4,128)S(1)} %bitcast.5, f32[128,512]{1,0:T(8,128)S(1)} %copy-done.2, ...), custom_call_target="tpu_custom_call" | custom-call | tf_op jit(solution)/shard_map/pallas_call | solution.py:404
  70.6 0.6 copy.19
  71.2 0.6 copy.20
Async XLA Ops:
  0.6 1.2 %copy-start = (f32[8,16384]{1,0:T(8,128)S(1)}, f32[8,16384]{1,0:T(8,128)}, u32[]{:S(2)}) copy-start(f32[8,16384]{1,0:T(8,128)} %coef.1) | copy-start | bytes 1572868
  0.6 1.2 %copy-start.5 = (f32[40,256]{1,0:T(8,128)S(1)}, f32[40,256]{1,0:T(8,128)}, u32[]{:S(2)}) copy-start(f32[40,256]{1,0:T(8,128)} %constant.20.clone.wts) | copy-start | bytes 122884
  1.8 1.0 %copy-start.1 = (f32[512,128]{1,0:T(8,128)S(1)}, f32[512,128]{1,0:T(8,128)}, u32[]{:S(2)}) copy-start(f32[512,128]{1,0:T(8,128)} %constant.15.clone.xtt) | copy-start | bytes 786436
  2.8 0.9 %copy-start.2 = (f32[128,512]{1,0:T(8,128)S(1)}, f32[128,512]{1,0:T(8,128)}, u32[]{:S(2)}) copy-start(f32[128,512]{1,0:T(8,128)} %constant.14.clone.xt) | copy-start | bytes 786436
  3.8 0.9 %copy-start.3 = (s32[1,32,544]{2,1,0:T(8,128)S(1)}, s32[1,32,544]{2,1,0:T(8,128)}, u32[]{:S(2)}) copy-start(s32[1,32,544]{2,1,0:T(8,128)} %param.14) | copy-start | bytes 208900
  4.6 0.9 %copy-start.4 = (s32[1,32,544]{2,1,0:T(8,128)S(1)}, s32[1,32,544]{2,1,0:T(8,128)}, u32[]{:S(2)}) copy-start(s32[1,32,544]{2,1,0:T(8,128)} %param.15) | copy-start | bytes 208900
  5.5 0.8 %copy-start.6 = (f32[80,40]{1,0:T(8,128)S(1)}, f32[80,40]{1,0:T(8,128)}, u32[]{:S(2)}) copy-start(f32[80,40]{1,0:T(8,128)} %constant.17.clone.vdv) | copy-start | bytes 38404
  6.3 0.7 %copy-start.7 = (f32[3,4,4,128]{3,2,1,0:T(4,128)S(1)}, f32[3,4,4,128]{3,2,1,0:T(4,128)}, u32[]{:S(2)}) copy-start(f32[3,4,4,128]{3,2,1,0:T(4,128)} %disp.1) | copy-start | bytes 73732
  7.0 0.7 %copy-start.8 = (f32[40,80]{1,0:T(8,128)S(1)}, f32[40,80]{1,0:T(8,128)}, u32[]{:S(2)}) copy-start(f32[40,80]{1,0:T(8,128)} %constant.19.clone.vdvt) | copy-start | bytes 38404
  7.8 0.7 %copy-start.9 = (f32[40,40]{1,0:T(8,128)S(1)}, f32[40,40]{1,0:T(8,128)}, u32[]{:S(2)}) copy-start(f32[40,40]{1,0:T(8,128)} %constant.18.clone.vvt) | copy-start | bytes 19204
  8.5 0.7 %copy-start.10 = (f32[40,40]{1,0:T(8,128)S(1)}, f32[40,40]{1,0:T(8,128)}, u32[]{:S(2)}) copy-start(f32[40,40]{1,0:T(8,128)} %constant.16.clone.vv) | copy-start | bytes 19204

commit v2 on v1

--- a/solution.py
+++ b/solution.py
@@ -2,6 +2,7 @@
 
 import jax
 import jax.numpy as jnp
+import ml_dtypes
 import numpy as np
 from jax import lax
 from jax.experimental import pallas as pl
@@ -12,11 +13,11 @@
 LS_STEPS = 4
 ROW = 8
 LO = 256
+GROUP = 4
 
 GAUSS_POINTS = np.array([0.5 - 0.5 * np.sqrt(0.6), 0.5, 0.5 + 0.5 * np.sqrt(0.6)])
 GAUSS_WEIGHTS = np.array([5.0 / 18.0, 8.0 / 18.0, 5.0 / 18.0])
 MESH = pl.DeviceIdType.MESH
-HIGHEST = lax.Precision.HIGHEST
 
 
 def basis_tables(elements, periodic):
@@ -67,32 +68,44 @@
         np.tile(GAUSS_WEIGHTS, ye),
         np.tile(GAUSS_WEIGHTS, xe),
     ).reshape(qr, qx)
-    tables = (
-        along_x,
-        along_x.T,
-        vv,
-        np.concatenate([vd, dv], axis=0),
-        vv.T,
-        np.concatenate([vd.T, dv.T], axis=1),
-        weights,
+    return (
+        thirds(along_x, 0),
+        thirds(along_x.T, 0),
+        thirds(vv, 1),
+        thirds(np.concatenate([vd, dv], axis=0), 1),
+        thirds(vv.T, 1),
+        thirds(np.concatenate([vd.T, dv.T], axis=1), 1),
+        weights.astype(np.float32),
     )
-    return tuple(np.ascontiguousarray(t).astype(np.float32) for t in tables)
+
+
+def thirds(table, axis):
+    head = table.astype(ml_dtypes.bfloat16)
+    tail = (table - head.astype(np.float64)).astype(ml_dtypes.bfloat16)
+    return np.concatenate([head, head, tail], axis=axis)
+
+
+def split(value, axis):
+    head = value.astype(jnp.bfloat16).astype(jnp.float32)
+    return jnp.concatenate([head, value - head, head], axis=axis).astype(jnp.bfloat16)
 
 
 def dot(a, b):
     return lax.dot_general(
-        a, b, (((1,), (0,)), ((), ())), precision=HIGHEST, preferred_element_type=jnp.float32
+        a, b, (((1,), (0,)), ((), ())), preferred_element_type=jnp.float32
     )
 
 
 def kernel(
     dims,
+    disp_in, coef_in, elem_in, point_in, coord_in,
+    xt_in, xtt_in, vv_in, vdv_in, vvt_in, vdvt_in, wts_in,
+    out, lc,
     disp, coef, elem, point, coord, xt, xtt, vv, vdv, vvt, vdvt, wts,
-    out, lc,
-    query, arrived, answer, found, tab32, tab, scat, fld, grad,
+    query, arrived, answer, found, tab, spots, scat, fld, grad,
     hy_send, hc_send, hz, hy, hc,
     ysend, csend, zrecv, yrecv, crecv, part, sums,
-    q_send, q_recv, f_send, f_recv, h_send, h_recv, x_send, x_recv, a_send, a_recv,
+    l_sem, q_send, q_recv, f_send, f_recv, h_send, h_recv, x_send, x_recv, a_send, a_recv,
 ):
     n_mesh, n_bg, nz, ny, qx = dims
     n = n_mesh * n_bg
@@ -117,6 +130,18 @@
     def wait_bytes(ref, sem):
         pltpu.make_async_copy(ref, ref, sem).wait()
 
+    local = [
+        pltpu.make_async_copy(src, dst, l_sem.at[i])
+        for i, (src, dst) in enumerate(
+            (
+                (elem_in, elem), (coord_in, coord), (disp_in, disp), (point_in, point),
+                (coef_in, coef), (xt_in, xt), (xtt_in, xtt), (vv_in, vv), (vdv_in, vdv),
+                (vvt_in, vvt), (vdvt_in, vdvt), (wts_in, wts),
+            )
+        )
+    ]
+    for copy in local:
+        copy.start()
     barrier = pltpu.get_barrier_semaphore()
 
     def greet(d, carry):
@@ -126,10 +151,13 @@
         return carry
 
     lax.fori_loop(1, n, greet, 0)
+    for copy in local[:3]:
+        copy.wait()
 
     def pack(o, carry):
         query[o, 0:1, :] = elem[pl.ds(o, 1), :].astype(jnp.float32)
-        query[o, 1:4, :] = coord[o]
+        for j in range(3):
+            query[o, 1 + j : 2 + j, :] = coord[j, pl.ds(o, 1), :]
         return carry
 
     lax.fori_loop(0, n, pack, 0)
@@ -155,48 +183,73 @@
     for copy in halo:
         copy.start()
 
-    for h in range(his):
-        tab32[8 * h : 8 * h + 8, :] = coef[:, LO * h : LO * h + LO]
-    whole = tab32[...]
-    top = whole.astype(jnp.bfloat16)
-    tab[:, :LO] = top
-    tab[:, LO:] = (whole - top.astype(jnp.float32)).astype(jnp.bfloat16)
+    local[3].wait()
+    qx_lanes = lax.broadcasted_iota(jnp.int32, (GROUP * cap, qxp), 1)
+    places = point[...].astype(jnp.float32)
+    levels = jnp.floor((places + 0.5) * (1.0 / qx))
+    offsets = jnp.transpose(places - levels * qx)
+    for g in range(n // GROUP):
+        column = jnp.concatenate(
+            [offsets[:, GROUP * g + j : GROUP * g + j + 1] for j in range(GROUP)], axis=0
+        ).astype(jnp.int32)
+        spots[g] = jnp.where(qx_lanes == column, 1.0, 0.0).astype(jnp.bfloat16)
+
+    local[4].wait()
+    for h in range(0, his, 2):
+        pair = jnp.concatenate(
+            [coef[:, LO * h : LO * (h + 1)], coef[:, LO * (h + 1) : LO * (h + 2)]], axis=0
+        )
+        top = pair.astype(jnp.bfloat16)
+        tab[8 * h : 8 * h + 16, :LO] = top
+        tab[8 * h : 8 * h + 16, LO:] = (pair - top.astype(jnp.float32)).astype(jnp.bfloat16)
     arrived[0] = query[me]
 
-    corner = lax.broadcasted_iota(jnp.int32, (8, cap), 0)
-    lo_rows = lax.broadcasted_iota(jnp.int32, (LO, cap), 0)
-
-    def serve(d):
-        ids = arrived[d, 0:1, :].astype(jnp.int32)
+    wide = GROUP * cap
+    corner = lax.broadcasted_iota(jnp.int32, (8, wide), 0)
+    lo_rows = lax.broadcasted_iota(jnp.int32, (LO, wide), 0)
+
+    def serve(g, carry):
+        first = g * GROUP
+        for j in range(GROUP):
+            d = first + j
+
+            @pl.when(d > 0)
+            def _():
+                source = device(lax.rem(me + n - d, n))
+                remote(query.at[0], arrived.at[d], q_send, q_recv.at[d], source).wait_recv()
+
+        asked = jnp.concatenate([arrived[first + j] for j in range(GROUP)], axis=1)
+        ids = asked[0:1].astype(jnp.int32)
         hi = lax.shift_right_logical(ids, LO.bit_length() - 1)
         lo = lax.bitwise_and(ids, LO - 1)
         one_hot = jnp.where(lo_rows == lo, 1.0, 0.0).astype(jnp.bfloat16)
-        one_hot = jnp.concatenate([one_hot, one_hot], axis=0)
-        rows = lax.dot_general(
-            tab[...], one_hot, (((1,), (0,)), ((), ())), preferred_element_type=jnp.float32
-        )
-        hi8 = jnp.broadcast_to(hi, (8, cap))
+        rows = dot(tab[...], jnp.concatenate([one_hot, one_hot], axis=0))
+        hi8 = jnp.broadcast_to(hi, (8, wide))
         chosen = rows[0:8]
         for h in range(1, his):
             chosen = jnp.where(hi8 == h, rows[8 * h : 8 * h + 8], chosen)
-        x, y, z = (arrived[d, j : j + 1, :] for j in (1, 2, 3))
+        x, y, z = (asked[j : j + 1] for j in (1, 2, 3))
         ax = jnp.where((corner & 1) != 0, x, 1.0 - x)
         ay = jnp.where((corner & 2) != 0, y, 1.0 - y)
         az = jnp.where((corner & 4) != 0, z, 1.0 - z)
-        lsize = jnp.sum(ax * ay * az * chosen, axis=0, keepdims=True)
-        return jnp.exp(-2.0 * lsize)
-
-    found[me] = serve(0)
-
-    def serve_remote(d, carry):
-        source = lax.rem(me + n - d, n)
-        remote(query.at[0], arrived.at[d], q_send, q_recv.at[d], device(source)).wait_recv()
-        answer[d] = serve(d)
-        remote(answer.at[d], found.at[me], f_send, f_recv, device(source)).start()
+        values = jnp.exp(-2.0 * jnp.sum(ax * ay * az * chosen, axis=0, keepdims=True))
+        for j in range(GROUP):
+            answer[first + j] = values[:, j * cap : (j + 1) * cap]
+        for j in range(GROUP):
+            d = first + j
+
+            @pl.when(d > 0)
+            def _():
+                source = device(lax.rem(me + n - d, n))
+                remote(answer.at[d], found.at[me], f_send, f_recv, source).start()
+
         return carry
 
-    lax.fori_loop(1, n, serve_remote, 0)
-
+    lax.fori_loop(0, n // GROUP, serve, 0)
+    found[me] = answer[0]
+
+    for copy in local[5:]:
+        copy.wait()
     for copy in halo:
         copy.wait()
     fld[...] = jnp.zeros_like(fld)
@@ -208,12 +261,12 @@
         fld[c, nz - 1, ny - 1 : ny, :] = hc[c : c + 1, :]
 
     def derivatives(flat):
-        along = dot(flat, xt[...])
+        along = dot(split(flat, 1), xt[...])
         result = []
         for c in range(3):
             rows = along[c * nz * ROW : (c + 1) * nz * ROW]
-            dx = dot(vv[...], rows[:, qxp:])
-            dyz = dot(vdv[...], rows[:, :qxp])
+            dx = dot(vv[...], split(rows[:, qxp:], 0))
+            dyz = dot(vdv[...], split(rows[:, :qxp], 0))
             result.append([dx, dyz[:qrp], dyz[qrp:]])
         return result
 
@@ -223,28 +276,24 @@
 
     wait_bytes(found.at[pl.ds(0, n - 1)], f_recv)
     scat[...] = jnp.zeros_like(scat)
-    hi_rows = lax.broadcasted_iota(jnp.int32, (qrp, cap), 0)
-    qx_rows = lax.broadcasted_iota(jnp.int32, (qxp, cap), 0)
-
-    def place(o, carry):
-        p = point[pl.ds(o, 1), :].astype(jnp.float32)
-        hi = jnp.floor((p + 0.5) * (1.0 / qx))
-        lo = (p - hi * qx).astype(jnp.int32)
-        mine = hi_rows == hi.astype(jnp.int32)
-        value = found[o]
+    hi_rows = lax.broadcasted_iota(jnp.int32, (qrp, wide), 0)
+
+    def place(g, carry):
+        first = g * GROUP
+        p = jnp.concatenate([point[pl.ds(first + j, 1), :] for j in range(GROUP)], axis=1)
+        level = jnp.floor((p.astype(jnp.float32) + 0.5) * (1.0 / qx)).astype(jnp.int32)
+        mine = hi_rows == level
+        value = jnp.concatenate([found[first + j] for j in range(GROUP)], axis=1)
         pieces = []
         for _ in range(3):
             piece = value.astype(jnp.bfloat16).astype(jnp.float32)
             value = value - piece
-            pieces.append(jnp.where(mine, piece, 0.0).astype(jnp.bfloat16))
-        left = jnp.concatenate(pieces, axis=0)
-        right = jnp.where(qx_rows == lo, 1.0, 0.0).astype(jnp.bfloat16)
-        scat[...] += lax.dot_general(
-            left, right, (((1,), (1,)), ((), ())), preferred_element_type=jnp.float32
-        )
+            pieces.append(jnp.where(mine, piece, 0.0))
+        left = jnp.concatenate(pieces, axis=0).astype(jnp.bfloat16)
+        scat[...] += dot(left, spots[g])
         return carry
 
-    lax.fori_loop(0, n, place, 0)
+    lax.fori_loop(0, n // GROUP, place, 0)
     scale = scat[:qrp] + scat[qrp : 2 * qrp] + scat[2 * qrp :]
     weights = wts[...]
     scale = jnp.where(weights > 0.0, scale, 0.0)
@@ -271,9 +320,9 @@
             for k in range(3):
                 total = sum(r0[min(k, l), max(k, l)] * jac[c][l] for l in range(3))
                 pulled.append(total * factor)
-            by_value = dot(vdvt[...], jnp.concatenate([pulled[1], pulled[2]], axis=0))
-            by_slope = dot(vvt[...], pulled[0])
-            node = dot(jnp.concatenate([by_value, by_slope], axis=1), xtt[...])
+            by_value = dot(vdvt[...], split(jnp.concatenate([pulled[1], pulled[2]], axis=0), 0))
+            by_slope = dot(vvt[...], split(pulled[0], 0))
+            node = dot(split(jnp.concatenate([by_value, by_slope], axis=1), 1), xtt[...])
             grad[turn, c] = node.reshape(nz, ROW, -1)
 
         for c in range(3):
@@ -348,8 +397,8 @@
             lc[turn : turn + 1, i : i + 1] = value[:, :1] / count
         fld[...] = fld[...] + t.reshape(1, 1, 1, 128) * direction
         if turn + 1 < PASSES:
-            wide = t[:, :1]
-            jac = [[jac[c][k] + wide * move[c][k] for k in range(3)] for c in range(3)]
+            step = t[:, :1]
+            jac = [[jac[c][k] + step * move[c][k] for k in range(3)] for c in range(3)]
 
     for c in range(3):
         for z in range(nz - 1):
@@ -376,13 +425,19 @@
     dims = (n_mesh, n_bg, nz, ny, 3 * xe)
     vmem = pl.BlockSpec(memory_space=pltpu.VMEM)
     dma = pltpu.SemaphoreType.DMA
+    operands = (
+        displacement, bg_coef, query_elem[0], query_point[0],
+        jnp.transpose(query_coord[0], (1, 0, 2)),
+        *(jnp.asarray(t) for t in tables),
+    )
     scratch = [
+        *(pltpu.VMEM(x.shape, x.dtype) for x in operands),
         pltpu.VMEM((n, 4, cap), f32),
         pltpu.VMEM((n, 4, cap), f32),
         pltpu.VMEM((n, 1, cap), f32),
         pltpu.VMEM((n, 1, cap), f32),
-        pltpu.VMEM((8 * his, LO), f32),
         pltpu.VMEM((8 * his, 2 * LO), jnp.bfloat16),
+        pltpu.VMEM((n // GROUP, GROUP * cap, qxp), jnp.bfloat16),
         pltpu.VMEM((3 * qrp, qxp), f32),
         pltpu.VMEM((3, nz, ROW, nx), f32),
         pltpu.VMEM((PASSES, 3, nz, ROW, nx), f32),
@@ -398,7 +453,7 @@
         pltpu.VMEM((PASSES, 4, 3, nx), f32),
         pltpu.VMEM((PASSES, 8, 128), f32),
         pltpu.VMEM((PASSES, n, 8, 128), f32),
-        dma, dma((n,)), dma, dma, dma((3,)), dma((3,)),
+        dma((12,)), dma, dma((n,)), dma, dma, dma((3,)), dma((3,)),
         dma((8 * PASSES,)), dma((8 * PASSES,)), dma((PASSES,)), dma((PASSES,)),
     ]
     out, lc = pl.pallas_call(
@@ -407,16 +462,13 @@
             jax.ShapeDtypeStruct(displacement.shape, f32),
             jax.ShapeDtypeStruct((PASSES, 5), f32),
         ),
-        in_specs=[vmem] * 12,
+        in_specs=[pl.BlockSpec(memory_space=pltpu.HBM)] * 12,
         out_specs=(vmem, vmem),
         scratch_shapes=scratch,
         compiler_params=pltpu.CompilerParams(
-            collective_id=0, has_side_effects=True, vmem_limit_bytes=48 * 2**20
+            collective_id=0, has_side_effects=True, vmem_limit_bytes=56 * 2**20
         ),
-    )(
-        displacement, bg_coef, query_elem[0], query_point[0], query_coord[0],
-        *(jnp.asarray(t) for t in tables),
-    )
+    )(*operands)
     return out, lc
 
 

time: 72.3 us -> 55 us (0.76)
  Pallas kernels: 61.3 us -> 52.2 us
  local copies, waits for them, and re-layouts: 9.72 us -> 1.91 us
    pallas_call x1, Pallas kernels: 61.3 us -> 52.2 us  [shards(): pl.pallas_call(functools.partial(kernel, dims), out_shape=(jax.ShapeDtype...]
    unnamed x25 -> x4, local copies, waits for them, and re-layouts: 9.72 us -> 1.91 us
where the time goes in v2:
time: 55 us; the launch traced here: 54.8 us
  Pallas kernels  52.2 us (95%)
  local copies, waits for them, and re-layouts  1.91 us (3%)
  between operations  0.65 us (1%)
    pallas_call x1, Pallas kernels, shards(): pl.pallas_call(functools.partial(kernel, dims), out_shape=(jax.ShapeDtype...  52.2 us
    unnamed x4, local copies, waits for them, and re-layouts  1.91 us

profile of v2, /device:TPU:0, one launch (start us, length us, event | category | flops | bytes accessed | tf_op | source)
XLA Modules:
  0.0 54.8 jit_solution(17353363676490034812)
XLA Ops:
  0.6 52.2 %shard_map.131 = (f32[3,4,4,128]{3,2,1,0:T(4,128)}, f32[2,5]{1,0:T(2,128)}) custom-call(f32[3,4,4,128]{3,2,1,0:T(4,128)} %disp_in.1, f32[8,16384]{1,0:T(8,128)} %coef_in.1, s32[32,544]{1,0:T(8,128)} %bitcast.6, s32[32,544]{1,0:T(8,128)} %bitcast.7, f32[3,32,544]{2,1,0:T(8,128)} %bitcast.5, bf16[384,512]{1,0:T(8,128)(2,1)} %constant.14.clone.xt_in, ...), custom_call_target="tpu_custom_call" | custom-call | tf_op jit(solution)/shard_map/pallas_call | solution.py:459
  52.9 0.0 copy-start
  52.9 1.3 %copy.16 = f32[3,4,4,128]{3,2,1,0:T(4,128)} copy(f32[3,4,4,128]{3,2,1,0:T(4,128)} %get-tuple-element.4) | data formatting | bytes 49152
  54.2 0.0 copy-done
  54.2 0.6 %copy.17 = f32[2,5]{1,0:T(2,128)} copy(f32[2,5]{1,0:T(2,128)S(1)} %copy-done) | data formatting | bytes 80
Async XLA Ops:
  52.9 1.4 %copy-start = (f32[2,5]{1,0:T(2,128)S(1)}, f32[2,5]{1,0:T(2,128)}, u32[]{:S(2)}) copy-start(f32[2,5]{1,0:T(2,128)} %get-tuple-element.5) | copy-start | bytes 124

commit v3 on v2

--- a/solution.py
+++ b/solution.py
@@ -102,7 +102,7 @@
     xt_in, xtt_in, vv_in, vdv_in, vvt_in, vdvt_in, wts_in,
     out, lc,
     disp, coef, elem, point, coord, xt, xtt, vv, vdv, vvt, vdvt, wts,
-    query, arrived, answer, found, tab, spots, scat, fld, grad,
+    query, arrived, answer, found, turned, tab, spots, scat, fld, grad,
     hy_send, hc_send, hz, hy, hc,
     ysend, csend, zrecv, yrecv, crecv, part, sums,
     l_sem, q_send, q_recv, f_send, f_recv, h_send, h_recv, x_send, x_recv, a_send, a_recv,
@@ -185,9 +185,14 @@
 
     local[3].wait()
     qx_lanes = lax.broadcasted_iota(jnp.int32, (GROUP * cap, qxp), 1)
-    places = point[...].astype(jnp.float32)
-    levels = jnp.floor((places + 0.5) * (1.0 / qx))
-    offsets = jnp.transpose(places - levels * qx)
+
+    def turn_rows(d, carry):
+        turned[pl.ds(d, 1), :] = point[pl.ds(lax.rem(me + d, n), 1), :].astype(jnp.float32)
+        return carry
+
+    lax.fori_loop(0, n, turn_rows, 0)
+    places = turned[...]
+    offsets = jnp.transpose(places - jnp.floor((places + 0.5) * (1.0 / qx)) * qx)
     for g in range(n // GROUP):
         column = jnp.concatenate(
             [offsets[:, GROUP * g + j : GROUP * g + j + 1] for j in range(GROUP)], axis=0
@@ -208,16 +213,43 @@
     corner = lax.broadcasted_iota(jnp.int32, (8, wide), 0)
     lo_rows = lax.broadcasted_iota(jnp.int32, (LO, wide), 0)
 
-    def serve(g, carry):
-        first = g * GROUP
+    hi_rows = lax.broadcasted_iota(jnp.int32, (qrp, wide), 0)
+
+    def source(d):
+        return device(lax.rem(me + n - d, n))
+
+    def await_queries(g):
         for j in range(GROUP):
-            d = first + j
+            d = g * GROUP + j
 
             @pl.when(d > 0)
             def _():
-                source = device(lax.rem(me + n - d, n))
-                remote(query.at[0], arrived.at[d], q_send, q_recv.at[d], source).wait_recv()
-
+                remote(query.at[0], arrived.at[d], q_send, q_recv.at[d], source(d)).wait_recv()
+
+    def await_answers(g):
+        for j in range(GROUP):
+            d = g * GROUP + j
+
+            @pl.when(d > 0)
+            def _():
+                remote(answer.at[0], found.at[d], f_send, f_recv.at[d], source(d)).wait_recv()
+
+    def reply(g):
+        for j in range(GROUP):
+            d = g * GROUP + j
+
+            @pl.when(d > 0)
+            def _():
+                remote(answer.at[d], found.at[d], f_send, f_recv.at[d], source(d)).start()
+
+            if j == 0:
+
+                @pl.when(d == 0)
+                def _():
+                    found[0] = answer[0]
+
+    def serve(g):
+        first = g * GROUP
         asked = jnp.concatenate([arrived[first + j] for j in range(GROUP)], axis=1)
         ids = asked[0:1].astype(jnp.int32)
         hi = lax.shift_right_logical(ids, LO.bit_length() - 1)
@@ -235,18 +267,44 @@
         values = jnp.exp(-2.0 * jnp.sum(ax * ay * az * chosen, axis=0, keepdims=True))
         for j in range(GROUP):
             answer[first + j] = values[:, j * cap : (j + 1) * cap]
-        for j in range(GROUP):
-            d = first + j
-
-            @pl.when(d > 0)
-            def _():
-                source = device(lax.rem(me + n - d, n))
-                remote(answer.at[d], found.at[me], f_send, f_recv, source).start()
-
-        return carry
-
-    lax.fori_loop(0, n // GROUP, serve, 0)
-    found[me] = answer[0]
+
+    def place(g):
+        first = g * GROUP
+        p = jnp.concatenate([turned[pl.ds(first + j, 1), :] for j in range(GROUP)], axis=1)
+        level = jnp.floor((p + 0.5) * (1.0 / qx)).astype(jnp.int32)
+        mine = hi_rows == level
+        value = jnp.concatenate([found[first + j] for j in range(GROUP)], axis=1)
+        pieces = []
+        for _ in range(3):
+            piece = value.astype(jnp.bfloat16).astype(jnp.float32)
+            value = value - piece
+            pieces.append(jnp.where(mine, piece, 0.0))
+        left = jnp.concatenate(pieces, axis=0).astype(jnp.bfloat16)
+        scat[...] += dot(left, spots[g])
+
+    def only_serve(g, carry):
+        await_queries(g)
+        serve(g)
+        reply(g)
+        return carry
+
+    def serve_and_place(g, carry):
+        await_queries(g)
+        await_answers(g - 2)
+        serve(g)
+        place(g - 2)
+        reply(g)
+        return carry
+
+    def only_place(g, carry):
+        await_answers(g)
+        place(g)
+        return carry
+
+    groups = n // GROUP
+    scat[...] = jnp.zeros_like(scat)
+    lax.fori_loop(0, 2, only_serve, 0)
+    lax.fori_loop(2, groups, serve_and_place, 0)
 
     for copy in local[5:]:
         copy.wait()
@@ -274,26 +332,7 @@
     for c in range(3):
         jac[c][c] = jac[c][c] + 1.0
 
-    wait_bytes(found.at[pl.ds(0, n - 1)], f_recv)
-    scat[...] = jnp.zeros_like(scat)
-    hi_rows = lax.broadcasted_iota(jnp.int32, (qrp, wide), 0)
-
-    def place(g, carry):
-        first = g * GROUP
-        p = jnp.concatenate([point[pl.ds(first + j, 1), :] for j in range(GROUP)], axis=1)
-        level = jnp.floor((p.astype(jnp.float32) + 0.5) * (1.0 / qx)).astype(jnp.int32)
-        mine = hi_rows == level
-        value = jnp.concatenate([found[first + j] for j in range(GROUP)], axis=1)
-        pieces = []
-        for _ in range(3):
-            piece = value.astype(jnp.bfloat16).astype(jnp.float32)
-            value = value - piece
-            pieces.append(jnp.where(mine, piece, 0.0))
-        left = jnp.concatenate(pieces, axis=0).astype(jnp.bfloat16)
-        scat[...] += dot(left, spots[g])
-        return carry
-
-    lax.fori_loop(0, n // GROUP, place, 0)
+    lax.fori_loop(groups - 2, groups, only_place, 0)
     scale = scat[:qrp] + scat[qrp : 2 * qrp] + scat[2 * qrp :]
     weights = wts[...]
     scale = jnp.where(weights > 0.0, scale, 0.0)
@@ -315,6 +354,7 @@
         gr = gram(jac, jac)
         r0 = {kl: gr[kl] * scale - (1.0 if kl[0] == kl[1] else 0.0) for kl in pairs}
         factor = (4.0 * weights) * scale
+        across = []
         for c in range(3):
             pulled = []
             for k in range(3):
@@ -322,8 +362,9 @@
                 pulled.append(total * factor)
             by_value = dot(vdvt[...], split(jnp.concatenate([pulled[1], pulled[2]], axis=0), 0))
             by_slope = dot(vvt[...], split(pulled[0], 0))
-            node = dot(split(jnp.concatenate([by_value, by_slope], axis=1), 1), xtt[...])
-            grad[turn, c] = node.reshape(nz, ROW, -1)
+            across.append(jnp.concatenate([by_value, by_slope], axis=1))
+        node = dot(split(jnp.concatenate(across, axis=0), 1), xtt[...])
+        grad[turn] = node.reshape(3, nz, ROW, -1)
 
         for c in range(3):
             for side, y in enumerate((0, ny - 1)):
@@ -436,6 +477,7 @@
         pltpu.VMEM((n, 4, cap), f32),
         pltpu.VMEM((n, 1, cap), f32),
         pltpu.VMEM((n, 1, cap), f32),
+        pltpu.VMEM((n, cap), f32),
         pltpu.VMEM((8 * his, 2 * LO), jnp.bfloat16),
         pltpu.VMEM((n // GROUP, GROUP * cap, qxp), jnp.bfloat16),
         pltpu.VMEM((3 * qrp, qxp), f32),
@@ -453,7 +495,7 @@
         pltpu.VMEM((PASSES, 4, 3, nx), f32),
         pltpu.VMEM((PASSES, 8, 128), f32),
         pltpu.VMEM((PASSES, n, 8, 128), f32),
-        dma((12,)), dma, dma((n,)), dma, dma, dma((3,)), dma((3,)),
+        dma((12,)), dma, dma((n,)), dma, dma((n,)), dma((3,)), dma((3,)),
         dma((8 * PASSES,)), dma((8 * PASSES,)), dma((PASSES,)), dma((PASSES,)),
     ]
     out, lc = pl.pallas_call(

time: 55 us -> 59.1 us (1.075)
  Pallas kernels: 52.2 us -> 56.3 us
    pallas_call x1, Pallas kernels: 52.2 us -> 56.3 us  [shards(): pl.pallas_call(functools.partial(kernel, dims), out_shape=(jax.ShapeDtype...]
where the time goes in v3:
time: 59.1 us; the launch traced here: 58.9 us
  Pallas kernels  56.3 us (95%)
  local copies, waits for them, and re-layouts  1.91 us (3%)
  between operations  0.65 us (1%)
    pallas_call x1, Pallas kernels, shards(): pl.pallas_call(functools.partial(kernel, dims), out_shape=(jax.ShapeDtype...  56.3 us
    unnamed x4, local copies, waits for them, and re-layouts  1.91 us

profile of v3, /device:TPU:0, one launch (start us, length us, event | category | flops | bytes accessed | tf_op | source)
XLA Modules:
  0.0 58.9 jit_solution(4303381178314420379)
XLA Ops:
  0.6 56.3 %shard_map.131 = (f32[3,4,4,128]{3,2,1,0:T(4,128)}, f32[2,5]{1,0:T(2,128)}) custom-call(f32[3,4,4,128]{3,2,1,0:T(4,128)} %disp_in.1, f32[8,16384]{1,0:T(8,128)} %coef_in.1, s32[32,544]{1,0:T(8,128)} %bitcast.6, s32[32,544]{1,0:T(8,128)} %bitcast.7, f32[3,32,544]{2,1,0:T(8,128)} %bitcast.5, bf16[384,512]{1,0:T(8,128)(2,1)} %constant.14.clone.xt_in, ...), custom_call_target="tpu_custom_call" | custom-call | tf_op jit(solution)/shard_map/pallas_call | solution.py:501
  57.0 0.0 copy-start
  57.0 1.3 %copy.16 = f32[3,4,4,128]{3,2,1,0:T(4,128)} copy(f32[3,4,4,128]{3,2,1,0:T(4,128)} %get-tuple-element.4) | data formatting | bytes 49152
  58.3 0.0 copy-done
  58.3 0.6 copy.17
Async XLA Ops:
  57.0 1.4 %copy-start = (f32[2,5]{1,0:T(2,128)S(1)}, f32[2,5]{1,0:T(2,128)}, u32[]{:S(2)}) copy-start(f32[2,5]{1,0:T(2,128)} %get-tuple-element.5) | copy-start | bytes 124

commit v4 on v2

--- a/solution.py
+++ b/solution.py
@@ -13,7 +13,6 @@
 LS_STEPS = 4
 ROW = 8
 LO = 256
-GROUP = 4
 
 GAUSS_POINTS = np.array([0.5 - 0.5 * np.sqrt(0.6), 0.5, 0.5 + 0.5 * np.sqrt(0.6)])
 GAUSS_WEIGHTS = np.array([5.0 / 18.0, 8.0 / 18.0, 5.0 / 18.0])
@@ -115,8 +114,21 @@
     zi, yi = lax.axis_index("mesh"), lax.axis_index("bg")
     me = zi * n_bg + yi
 
-    def device(index):
-        return (lax.div(index, n_bg), lax.rem(index, n_bg))
+    group = n_bg
+    ahead = [lax.rem(yi + dy, n_bg) for dy in range(n_bg)]
+    behind = [lax.rem(yi + (n_bg - dy), n_bg) for dy in range(n_bg)]
+
+    def each_partner(act):
+        for dy in range(1, n_bg):
+            act(dy, zi * n_bg + ahead[dy], (zi, ahead[dy]))
+
+        def row(dz, carry):
+            z = lax.rem(zi + dz, n_mesh)
+            for dy in range(n_bg):
+                act(dz * n_bg + dy, z * n_bg + ahead[dy], (z, ahead[dy]))
+            return carry
+
+        lax.fori_loop(1, n_mesh, row, 0)
 
     def near(dz, dy):
         return (lax.rem(zi + n_mesh + dz, n_mesh), lax.rem(yi + n_bg + dy, n_bg))
@@ -144,13 +156,10 @@
         copy.start()
     barrier = pltpu.get_barrier_semaphore()
 
-    def greet(d, carry):
-        pl.semaphore_signal(
-            barrier, inc=1, device_id=device(lax.rem(me + d, n)), device_id_type=MESH
-        )
-        return carry
-
-    lax.fori_loop(1, n, greet, 0)
+    def greet(slot, index, target):
+        pl.semaphore_signal(barrier, inc=1, device_id=target, device_id_type=MESH)
+
+    each_partner(greet)
     for copy in local[:3]:
         copy.wait()
 
@@ -167,14 +176,10 @@
         hc_send[c : c + 1, :] = disp[c, 0, 0:1, :]
     pl.semaphore_wait(barrier, n - 1)
 
-    def send_query(d, carry):
-        target = lax.rem(me + d, n)
-        remote(
-            query.at[target], arrived.at[d], q_send, q_recv.at[d], device(target)
-        ).start()
-        return carry
-
-    lax.fori_loop(1, n, send_query, 0)
+    def send_query(slot, index, target):
+        remote(query.at[index], arrived.at[slot], q_send, q_recv.at[slot], target).start()
+
+    each_partner(send_query)
     halo = [
         remote(disp.at[:, 0], hz, h_send.at[0], h_recv.at[0], near(-1, 0)),
         remote(hy_send, hy, h_send.at[1], h_recv.at[1], near(0, -1)),
@@ -184,15 +189,16 @@
         copy.start()
 
     local[3].wait()
-    qx_lanes = lax.broadcasted_iota(jnp.int32, (GROUP * cap, qxp), 1)
+    one, zero = jnp.bfloat16(1.0), jnp.bfloat16(0.0)
+    qx_lanes = lax.broadcasted_iota(jnp.int32, (group * cap, qxp), 1).astype(jnp.bfloat16)
     places = point[...].astype(jnp.float32)
     levels = jnp.floor((places + 0.5) * (1.0 / qx))
     offsets = jnp.transpose(places - levels * qx)
-    for g in range(n // GROUP):
+    for g in range(n // group):
         column = jnp.concatenate(
-            [offsets[:, GROUP * g + j : GROUP * g + j + 1] for j in range(GROUP)], axis=0
-        ).astype(jnp.int32)
-        spots[g] = jnp.where(qx_lanes == column, 1.0, 0.0).astype(jnp.bfloat16)
+            [offsets[:, group * g + j : group * g + j + 1] for j in range(group)], axis=0
+        ).astype(jnp.bfloat16)
+        spots[g] = jnp.where(qx_lanes == column, one, zero)
 
     local[4].wait()
     for h in range(0, his, 2):
@@ -204,25 +210,34 @@
         tab[8 * h : 8 * h + 16, LO:] = (pair - top.astype(jnp.float32)).astype(jnp.bfloat16)
     arrived[0] = query[me]
 
-    wide = GROUP * cap
+    wide = group * cap
     corner = lax.broadcasted_iota(jnp.int32, (8, wide), 0)
-    lo_rows = lax.broadcasted_iota(jnp.int32, (LO, wide), 0)
+    lo_rows = lax.broadcasted_iota(jnp.int32, (LO, wide), 0).astype(jnp.bfloat16)
 
     def serve(g, carry):
-        first = g * GROUP
-        for j in range(GROUP):
+        first = g * group
+        back = lax.rem(zi + (n_mesh - g), n_mesh)
+
+        def await_query(j):
             d = first + j
-
-            @pl.when(d > 0)
-            def _():
-                source = device(lax.rem(me + n - d, n))
-                remote(query.at[0], arrived.at[d], q_send, q_recv.at[d], source).wait_recv()
-
-        asked = jnp.concatenate([arrived[first + j] for j in range(GROUP)], axis=1)
+            remote(
+                query.at[0], arrived.at[d], q_send, q_recv.at[d], (back, behind[j])
+            ).wait_recv()
+
+        def reply(j):
+            remote(
+                answer.at[first + j], found.at[me], f_send, f_recv, (back, behind[j])
+            ).start()
+
+        for j in range(1, group):
+            await_query(j)
+        pl.when(g > 0)(functools.partial(await_query, 0))
+
+        asked = jnp.concatenate([arrived[first + j] for j in range(group)], axis=1)
         ids = asked[0:1].astype(jnp.int32)
         hi = lax.shift_right_logical(ids, LO.bit_length() - 1)
-        lo = lax.bitwise_and(ids, LO - 1)
-        one_hot = jnp.where(lo_rows == lo, 1.0, 0.0).astype(jnp.bfloat16)
+        lo = lax.bitwise_and(ids, LO - 1).astype(jnp.float32).astype(jnp.bfloat16)
+        one_hot = jnp.where(lo_rows == lo, one, zero)
         rows = dot(tab[...], jnp.concatenate([one_hot, one_hot], axis=0))
         hi8 = jnp.broadcast_to(hi, (8, wide))
         chosen = rows[0:8]
@@ -233,19 +248,14 @@
         ay = jnp.where((corner & 2) != 0, y, 1.0 - y)
         az = jnp.where((corner & 4) != 0, z, 1.0 - z)
         values = jnp.exp(-2.0 * jnp.sum(ax * ay * az * chosen, axis=0, keepdims=True))
-        for j in range(GROUP):
+        for j in range(group):
             answer[first + j] = values[:, j * cap : (j + 1) * cap]
-        for j in range(GROUP):
-            d = first + j
-
-            @pl.when(d > 0)
-            def _():
-                source = device(lax.rem(me + n - d, n))
-                remote(answer.at[d], found.at[me], f_send, f_recv, source).start()
-
+        for j in range(1, group):
+            reply(j)
+        pl.when(g > 0)(functools.partial(reply, 0))
         return carry
 
-    lax.fori_loop(0, n // GROUP, serve, 0)
+    lax.fori_loop(0, n // group, serve, 0)
     found[me] = answer[0]
 
     for copy in local[5:]:
@@ -279,11 +289,11 @@
     hi_rows = lax.broadcasted_iota(jnp.int32, (qrp, wide), 0)
 
     def place(g, carry):
-        first = g * GROUP
-        p = jnp.concatenate([point[pl.ds(first + j, 1), :] for j in range(GROUP)], axis=1)
+        first = g * group
+        p = jnp.concatenate([point[pl.ds(first + j, 1), :] for j in range(group)], axis=1)
         level = jnp.floor((p.astype(jnp.float32) + 0.5) * (1.0 / qx)).astype(jnp.int32)
         mine = hi_rows == level
-        value = jnp.concatenate([found[first + j] for j in range(GROUP)], axis=1)
+        value = jnp.concatenate([found[first + j] for j in range(group)], axis=1)
         pieces = []
         for _ in range(3):
             piece = value.astype(jnp.bfloat16).astype(jnp.float32)
@@ -293,7 +303,7 @@
         scat[...] += dot(left, spots[g])
         return carry
 
-    lax.fori_loop(0, n // GROUP, place, 0)
+    lax.fori_loop(0, n // group, place, 0)
     scale = scat[:qrp] + scat[qrp : 2 * qrp] + scat[2 * qrp :]
     weights = wts[...]
     scale = jnp.where(weights > 0.0, scale, 0.0)
@@ -315,6 +325,7 @@
         gr = gram(jac, jac)
         r0 = {kl: gr[kl] * scale - (1.0 if kl[0] == kl[1] else 0.0) for kl in pairs}
         factor = (4.0 * weights) * scale
+        across = []
         for c in range(3):
             pulled = []
             for k in range(3):
@@ -322,8 +333,9 @@
                 pulled.append(total * factor)
             by_value = dot(vdvt[...], split(jnp.concatenate([pulled[1], pulled[2]], axis=0), 0))
             by_slope = dot(vvt[...], split(pulled[0], 0))
-            node = dot(split(jnp.concatenate([by_value, by_slope], axis=1), 1), xtt[...])
-            grad[turn, c] = node.reshape(nz, ROW, -1)
+            across.append(jnp.concatenate([by_value, by_slope], axis=1))
+        node = dot(split(jnp.concatenate(across, axis=0), 1), xtt[...])
+        grad[turn] = node.reshape(3, nz, ROW, -1)
 
         for c in range(3):
             for side, y in enumerate((0, ny - 1)):
@@ -373,14 +385,12 @@
         part[turn] = mine
         sums[turn, me] = mine
 
-        def share(d, carry, turn=turn):
+        def share(slot, index, target, turn=turn):
             remote(
-                part.at[turn], sums.at[turn, me], a_send.at[turn], a_recv.at[turn],
-                device(lax.rem(me + d, n)),
+                part.at[turn], sums.at[turn, me], a_send.at[turn], a_recv.at[turn], target
             ).start()
-            return carry
-
-        lax.fori_loop(1, n, share, 0)
+
+        each_partner(share)
         wait_bytes(sums.at[turn, pl.ds(0, n - 1)], a_recv.at[turn])
         totals = jnp.sum(jnp.sum(sums[turn], axis=0), axis=1, keepdims=True)
         d00, d01, d02, d12, d22, gn = (
@@ -402,7 +412,8 @@
 
     for c in range(3):
         for z in range(nz - 1):
-            out[c, z] = fld[c, z, 0 : ny - 1, :]
+            at = (c * (nz - 1) + z) * (ny - 1)
+            out[at : at + ny - 1, :] = fld[c, z, 0 : ny - 1, :]
 
     wait_bytes(query.at[pl.ds(0, n - 1)], q_send)
     wait_bytes(answer.at[pl.ds(0, n - 1)], f_send)
@@ -437,7 +448,7 @@
         pltpu.VMEM((n, 1, cap), f32),
         pltpu.VMEM((n, 1, cap), f32),
         pltpu.VMEM((8 * his, 2 * LO), jnp.bfloat16),
-        pltpu.VMEM((n // GROUP, GROUP * cap, qxp), jnp.bfloat16),
+        pltpu.VMEM((n_mesh, n_bg * cap, qxp), jnp.bfloat16),
         pltpu.VMEM((3 * qrp, qxp), f32),
         pltpu.VMEM((3, nz, ROW, nx), f32),
         pltpu.VMEM((PASSES, 3, nz, ROW, nx), f32),
@@ -459,7 +470,7 @@
     out, lc = pl.pallas_call(
         functools.partial(kernel, dims),
         out_shape=(
-            jax.ShapeDtypeStruct(displacement.shape, f32),
+            jax.ShapeDtypeStruct((3 * nz0 * ny0, nx), f32),
             jax.ShapeDtypeStruct((PASSES, 5), f32),
         ),
         in_specs=[pl.BlockSpec(memory_space=pltpu.HBM)] * 12,
@@ -469,7 +480,7 @@
             collective_id=0, has_side_effects=True, vmem_limit_bytes=56 * 2**20
         ),
     )(*operands)
-    return out, lc
+    return out.reshape(displacement.shape), lc
 
 
 def solution(mesh):

time: 55 us -> 54.3 us (0.987)
  Pallas kernels: 52.2 us -> 51.6 us
    pallas_call x1, Pallas kernels: 52.2 us -> 51.6 us  [shards(): pl.pallas_call(functools.partial(kernel, dims), out_shape=(jax.ShapeDtype...]
where the time goes in v4:
time: 54.3 us; the launch traced here: 54.1 us
  Pallas kernels  51.6 us (95%)
  local copies, waits for them, and re-layouts  1.91 us (4%)
  between operations  0.65 us (1%)
    pallas_call x1, Pallas kernels, shards(): pl.pallas_call(functools.partial(kernel, dims), out_shape=(jax.ShapeDtype...  51.6 us
    unnamed x4, local copies, waits for them, and re-layouts  1.91 us

profile of v4, /device:TPU:0, one launch (start us, length us, event | category | flops | bytes accessed | tf_op | source)
XLA Modules:
  0.0 54.1 jit_solution(8052910591726649955)
XLA Ops:
  0.6 51.6 %shard_map.131 = (f32[48,128]{1,0:T(8,128)}, f32[2,5]{1,0:T(2,128)}) custom-call(f32[3,4,4,128]{3,2,1,0:T(4,128)} %disp_in.1, f32[8,16384]{1,0:T(8,128)} %coef_in.1, s32[32,544]{1,0:T(8,128)} %bitcast.7, s32[32,544]{1,0:T(8,128)} %bitcast.8, f32[3,32,544]{2,1,0:T(8,128)} %bitcast.6, bf16[384,512]{1,0:T(8,128)(2,1)} %constant.14.clone.xt_in, ...), custom_call_target="tpu_custom_call" | custom-call | tf_op jit(solution)/shard_map/pallas_call | solution.py:470
  52.2 0.0 copy-start
  52.2 1.3 %copy.16 = f32[3,4,4,128]{3,2,1,0:T(4,128)} copy(f32[3,4,4,128]{3,2,1,0:T(4,128)} %bitcast.9) | data formatting | bytes 49152
  53.5 0.0 copy-done
  53.6 0.6 %copy.17 = f32[2,5]{1,0:T(2,128)} copy(f32[2,5]{1,0:T(2,128)S(1)} %copy-done) | data formatting | bytes 80
Async XLA Ops:
  52.2 1.4 %copy-start = (f32[2,5]{1,0:T(2,128)S(1)}, f32[2,5]{1,0:T(2,128)}, u32[]{:S(2)}) copy-start(f32[2,5]{1,0:T(2,128)} %get-tuple-element.9) | copy-start | bytes 124

commit v5 on v4

--- a/solution.py
+++ b/solution.py
@@ -13,6 +13,7 @@
 LS_STEPS = 4
 ROW = 8
 LO = 256
+CHUNK = 768
 
 GAUSS_POINTS = np.array([0.5 - 0.5 * np.sqrt(0.6), 0.5, 0.5 + 0.5 * np.sqrt(0.6)])
 GAUSS_WEIGHTS = np.array([5.0 / 18.0, 8.0 / 18.0, 5.0 / 18.0])
@@ -237,12 +238,17 @@
         ids = asked[0:1].astype(jnp.int32)
         hi = lax.shift_right_logical(ids, LO.bit_length() - 1)
         lo = lax.bitwise_and(ids, LO - 1).astype(jnp.float32).astype(jnp.bfloat16)
-        one_hot = jnp.where(lo_rows == lo, one, zero)
-        rows = dot(tab[...], jnp.concatenate([one_hot, one_hot], axis=0))
-        hi8 = jnp.broadcast_to(hi, (8, wide))
-        chosen = rows[0:8]
-        for h in range(1, his):
-            chosen = jnp.where(hi8 == h, rows[8 * h : 8 * h + 8], chosen)
+        picked = []
+        for at in range(0, wide, CHUNK):
+            end = min(at + CHUNK, wide)
+            one_hot = jnp.where(lo_rows[:, at:end] == lo[:, at:end], one, zero)
+            rows = dot(tab[...], jnp.concatenate([one_hot, one_hot], axis=0))
+            hi8 = jnp.broadcast_to(hi[:, at:end], (8, end - at))
+            chosen = rows[0:8]
+            for h in range(1, his):
+                chosen = jnp.where(hi8 == h, rows[8 * h : 8 * h + 8], chosen)
+            picked.append(chosen)
+        chosen = jnp.concatenate(picked, axis=1)
         x, y, z = (asked[j : j + 1] for j in (1, 2, 3))
         ax = jnp.where((corner & 1) != 0, x, 1.0 - x)
         ay = jnp.where((corner & 2) != 0, y, 1.0 - y)

time: 54.3 us -> 54.3 us (level)
  no operation moved by 1% of the time
where the time goes in v5:
time: 54.3 us; the launch traced here: 54.1 us
  Pallas kernels  51.6 us (95%)
  local copies, waits for them, and re-layouts  1.91 us (4%)
  between operations  0.65 us (1%)
    pallas_call x1, Pallas kernels, shards(): pl.pallas_call(functools.partial(kernel, dims), out_shape=(jax.ShapeDtype...  51.6 us
    unnamed x4, local copies, waits for them, and re-layouts  1.91 us

profile of v5, /device:TPU:0, one launch (start us, length us, event | category | flops | bytes accessed | tf_op | source)
XLA Modules:
  0.0 54.1 jit_solution(8052910591726649955)
XLA Ops:
  0.6 51.6 %shard_map.131 = (f32[48,128]{1,0:T(8,128)}, f32[2,5]{1,0:T(2,128)}) custom-call(f32[3,4,4,128]{3,2,1,0:T(4,128)} %disp_in.1, f32[8,16384]{1,0:T(8,128)} %coef_in.1, s32[32,544]{1,0:T(8,128)} %bitcast.7, s32[32,544]{1,0:T(8,128)} %bitcast.8, f32[3,32,544]{2,1,0:T(8,128)} %bitcast.6, bf16[384,512]{1,0:T(8,128)(2,1)} %constant.14.clone.xt_in, ...), custom_call_target="tpu_custom_call" | custom-call | tf_op jit(solution)/shard_map/pallas_call | solution.py:476
  52.2 0.0 copy-start
  52.2 1.3 %copy.16 = f32[3,4,4,128]{3,2,1,0:T(4,128)} copy(f32[3,4,4,128]{3,2,1,0:T(4,128)} %bitcast.9) | data formatting | bytes 49152
  53.5 0.0 copy-done
  53.6 0.6 %copy.17 = f32[2,5]{1,0:T(2,128)} copy(f32[2,5]{1,0:T(2,128)S(1)} %copy-done) | data formatting | bytes 80
Async XLA Ops:
  52.2 1.4 %copy-start = (f32[2,5]{1,0:T(2,128)S(1)}, f32[2,5]{1,0:T(2,128)}, u32[]{:S(2)}) copy-start(f32[2,5]{1,0:T(2,128)} %get-tuple-element.9) | copy-start | bytes 124

commit v6 on v5

--- a/solution.py
+++ b/solution.py
@@ -12,7 +12,7 @@
 PASSES = 2
 LS_STEPS = 4
 ROW = 8
-LO = 256
+LO = 128
 CHUNK = 768
 
 GAUSS_POINTS = np.array([0.5 - 0.5 * np.sqrt(0.6), 0.5, 0.5 + 0.5 * np.sqrt(0.6)])

time: 54.3 us -> 54.4 us (level)
  no operation moved by 1% of the time
where the time goes in v6:
time: 54.4 us; the launch traced here: 54.2 us
  Pallas kernels  51.7 us (95%)
  local copies, waits for them, and re-layouts  1.91 us (4%)
  between operations  0.65 us (1%)
    pallas_call x1, Pallas kernels, shards(): pl.pallas_call(functools.partial(kernel, dims), out_shape=(jax.ShapeDtype...  51.7 us
    unnamed x4, local copies, waits for them, and re-layouts  1.91 us

profile of v6, /device:TPU:0, one launch (start us, length us, event | category | flops | bytes accessed | tf_op | source)
XLA Modules:
  0.0 54.2 jit_solution(14769675813910833641)
XLA Ops:
  0.6 51.7 %shard_map.131 = (f32[48,128]{1,0:T(8,128)}, f32[2,5]{1,0:T(2,128)}) custom-call(f32[3,4,4,128]{3,2,1,0:T(4,128)} %disp_in.1, f32[8,16384]{1,0:T(8,128)} %coef_in.1, s32[32,544]{1,0:T(8,128)} %bitcast.7, s32[32,544]{1,0:T(8,128)} %bitcast.8, f32[3,32,544]{2,1,0:T(8,128)} %bitcast.6, bf16[384,512]{1,0:T(8,128)(2,1)} %constant.14.clone.xt_in, ...), custom_call_target="tpu_custom_call" | custom-call | tf_op jit(solution)/shard_map/pallas_call | solution.py:476
  52.3 0.0 copy-start
  52.3 1.3 %copy.16 = f32[3,4,4,128]{3,2,1,0:T(4,128)} copy(f32[3,4,4,128]{3,2,1,0:T(4,128)} %bitcast.9) | data formatting | bytes 49152
  53.7 0.0 copy-done
  53.7 0.6 %copy.17 = f32[2,5]{1,0:T(2,128)} copy(f32[2,5]{1,0:T(2,128)S(1)} %copy-done) | data formatting | bytes 80
Async XLA Ops:
  52.3 1.4 %copy-start = (f32[2,5]{1,0:T(2,128)S(1)}, f32[2,5]{1,0:T(2,128)}, u32[]{:S(2)}) copy-start(f32[2,5]{1,0:T(2,128)} %get-tuple-element.9) | copy-start | bytes 124

commit v7 on v5

--- a/solution.py
+++ b/solution.py
@@ -301,7 +301,7 @@
         mine = hi_rows == level
         value = jnp.concatenate([found[first + j] for j in range(group)], axis=1)
         pieces = []
-        for _ in range(3):
+        for _ in range(2):
             piece = value.astype(jnp.bfloat16).astype(jnp.float32)
             value = value - piece
             pieces.append(jnp.where(mine, piece, 0.0))
@@ -310,7 +310,7 @@
         return carry
 
     lax.fori_loop(0, n // group, place, 0)
-    scale = scat[:qrp] + scat[qrp : 2 * qrp] + scat[2 * qrp :]
+    scale = scat[:qrp] + scat[qrp:]
     weights = wts[...]
     scale = jnp.where(weights > 0.0, scale, 0.0)
 
@@ -455,7 +455,7 @@
         pltpu.VMEM((n, 1, cap), f32),
         pltpu.VMEM((8 * his, 2 * LO), jnp.bfloat16),
         pltpu.VMEM((n_mesh, n_bg * cap, qxp), jnp.bfloat16),
-        pltpu.VMEM((3 * qrp, qxp), f32),
+        pltpu.VMEM((2 * qrp, qxp), f32),
         pltpu.VMEM((3, nz, ROW, nx), f32),
         pltpu.VMEM((PASSES, 3, nz, ROW, nx), f32),
         pltpu.VMEM((3, nz0, nx), f32),

time: 54.3 us -> 54.2 us (level)
  no operation moved by 1% of the time
where the time goes in v7:
time: 54.2 us; the launch traced here: 54 us
  Pallas kernels  51.4 us (95%)
  local copies, waits for them, and re-layouts  1.91 us (4%)
  between operations  0.65 us (1%)
    pallas_call x1, Pallas kernels, shards(): pl.pallas_call(functools.partial(kernel, dims), out_shape=(jax.ShapeDtype...  51.4 us
    unnamed x4, local copies, waits for them, and re-layouts  1.91 us

profile of v7, /device:TPU:0, one launch (start us, length us, event | category | flops | bytes accessed | tf_op | source)
XLA Modules:
  0.0 54.0 jit_solution(11836206511141193341)
XLA Ops:
  0.6 51.4 %shard_map.131 = (f32[48,128]{1,0:T(8,128)}, f32[2,5]{1,0:T(2,128)}) custom-call(f32[3,4,4,128]{3,2,1,0:T(4,128)} %disp_in.1, f32[8,16384]{1,0:T(8,128)} %coef_in.1, s32[32,544]{1,0:T(8,128)} %bitcast.7, s32[32,544]{1,0:T(8,128)} %bitcast.8, f32[3,32,544]{2,1,0:T(8,128)} %bitcast.6, bf16[384,512]{1,0:T(8,128)(2,1)} %constant.14.clone.xt_in, ...), custom_call_target="tpu_custom_call" | custom-call | tf_op jit(solution)/shard_map/pallas_call | solution.py:476
  52.1 0.0 copy-start
  52.1 1.3 %copy.16 = f32[3,4,4,128]{3,2,1,0:T(4,128)} copy(f32[3,4,4,128]{3,2,1,0:T(4,128)} %bitcast.9) | data formatting | bytes 49152
  53.4 0.0 copy-done
  53.4 0.6 %copy.17 = f32[2,5]{1,0:T(2,128)} copy(f32[2,5]{1,0:T(2,128)S(1)} %copy-done) | data formatting | bytes 80
Async XLA Ops:
  52.1 1.4 %copy-start = (f32[2,5]{1,0:T(2,128)S(1)}, f32[2,5]{1,0:T(2,128)}, u32[]{:S(2)}) copy-start(f32[2,5]{1,0:T(2,128)} %get-tuple-element.9) | copy-start | bytes 124
